TPU v7x, 128 devices: a whole 4x4x4 slice. The times are simulated.
128 devices in a mesh: ctx: 8 (over x, core), exp: 16 (over z, y).
Axes of the slice: x: 4, y: 4, z: 4, core: 2. Of those that a mesh axis runs over, the one named last changes fastest.
Arguments:
- hidden_in: bfloat16 [16384, 3584], P(('ctx', 'exp')), may hold values from -6 to 6
- queries: bfloat16 [16384, 3584], P(('ctx', 'exp')), may hold values from -21 to 21
- key_rows: bfloat16 [16384, 512], P(('ctx', 'exp')), may hold values from -6 to 6
- value_rows: bfloat16 [16384, 512], P(('ctx', 'exp')), may hold values from -6 to 6
- document_ids: int32 [16384], P(('ctx', 'exp')), may hold values from 0 to 127, never falling along the last dimension, each value on 1 to 384 neighbouring positions
- norm_gain: float32 [3584], replicated, may hold values from 0.1 to 1.9
- w_gate: bfloat16 [128, 3584, 640], P(('ctx', 'exp')), may hold values from -0.09375 to 0.09375
- w_up: bfloat16 [128, 3584, 640], P(('ctx', 'exp')), may hold values from -0.09375 to 0.09375
- w_down: bfloat16 [128, 640, 3584], P(('ctx', 'exp')), may hold values from -0.15625 to 0.15625
- expert_ids: int32 [16384, 8], P(('ctx', 'exp')), may hold values from 0 to 63, all different within a row; in each aligned block of 128 rows (0 to 127, 128 to 255, ...) at most 17 rows name the same one
- route_weights: float32 [16384, 8], P(('ctx', 'exp')), may hold values from 0.05 to 0.6
Outputs:
- layer_out: bfloat16 [16384, 3584], P(('ctx', 'exp'))
Inputs may be any that keep to these rules, and one draw needn't show every extreme that they name: `document_ids`: document ids never fall along the row; each document has 1 to 384 positions and one has exactly 384. `expert_ids`: the 8 ids of a token are distinct. Among the 128 tokens of one device (aligned blocks of the row) no expert is named more than 17 times, and in every draw some expert is named exactly 17 times in some block.
All inputs are finite; a program needn't handle non-finite values.
Results may differ from a plain program's by a relative error of at most 0.015.
Values may be sent and summed in bfloat16 or wider, within the bound.
A program may use at most 192 MiB of HBM per device.

v0:
```python
import jax
import jax.numpy as jnp
from jax import lax
from jax.sharding import PartitionSpec as P

D = 3584
KV_HEADS = 4
HEAD_DIM = 128
TOPK = 8
WINDOW = 4
GROUP = 7


masked_score = -1e30


def from_behind(value, axis, steps):
    count = lax.axis_size(axis)
    initial, last = (max(0, -steps), min(count, count - steps))
    return lax.ppermute(value, axis, [(source, source + steps) for source in range(initial, last)])


def join_blocks(earlier, later):
    return tuple(
        (
            jnp.concatenate([first_part, second_part], 0)
            for first_part, second_part in zip(earlier, later)
        )
    )


def tile_scores(query_heads, key_tile, scale_factor):
    key_heads = key_tile.reshape(key_tile.shape[0], KV_HEADS, HEAD_DIM)
    return (
        jnp.einsum("qkgd,pkd->kgqp", query_heads, key_heads, preferred_element_type=jnp.float32)
        * scale_factor
    )


def tile_context(prob_tile, value_tile):
    value_heads = value_tile.reshape(value_tile.shape[0], KV_HEADS, HEAD_DIM)
    return jnp.einsum("kgqp,pkd->qkgd", prob_tile, value_heads, preferred_element_type=jnp.float32)


def send_out(buffer):
    device_count = buffer.shape[0]
    arrived = lax.all_to_all(buffer, ("ctx", "exp"), split_axis=0, concat_axis=0, tiled=True)
    return arrived


def send_back(buffer):
    device_count = buffer.shape[0]
    arrived = lax.all_to_all(buffer, ("ctx", "exp"), split_axis=0, concat_axis=0, tiled=True)
    return arrived


def on_device(
    hidden_in,
    queries,
    key_rows,
    value_rows,
    document_ids,
    norm_gain,
    w_gate,
    w_up,
    w_down,
    expert_ids,
    route_weights,
):
    token_count = hidden_in.shape[0]
    device_count = lax.axis_size(("ctx", "exp"))
    device_rank = lax.axis_index(("ctx", "exp"))
    code_own = (document_ids + 1).astype(jnp.bfloat16)[:, None]
    own_block = (key_rows, value_rows, code_own)
    window_blocks = own_block
    for distance in range(1, WINDOW):
        arrived = from_behind((key_rows, value_rows, code_own), ("ctx", "exp"), distance)
        window_blocks = join_blocks(arrived, window_blocks)
    key_window, value_window, code_window = window_blocks
    window_len = key_window.shape[0]
    query_pos = device_rank * token_count + jnp.arange(token_count, dtype=jnp.int32)
    key_pos = (device_rank - (WINDOW - 1)) * token_count + jnp.arange(window_len, dtype=jnp.int32)
    query_code = (document_ids + 1).astype(jnp.float32)
    key_code = code_window[:, 0].astype(jnp.float32)
    visible = (query_code[:, None] == key_code[None, :]) & (key_pos[None, :] <= query_pos[:, None])
    query_heads = queries.reshape(token_count, KV_HEADS, GROUP, HEAD_DIM)
    scale_factor = HEAD_DIM ** (-0.5)
    scores = jnp.where(
        visible[None, None], tile_scores(query_heads, key_window, scale_factor), masked_score
    )
    top_score = jnp.max(scores, 3, keepdims=True)
    exps = jnp.exp(scores - top_score)
    probs = (exps / jnp.sum(exps, 3, keepdims=True)).astype(jnp.bfloat16)
    context_sum = tile_context(probs, value_window)
    context = context_sum.reshape(token_count, D).astype(jnp.bfloat16)
    resid = (hidden_in.astype(jnp.float32) + context.astype(jnp.float32)).astype(jnp.bfloat16)
    resid_f = resid.astype(jnp.float32)
    inverse = lax.rsqrt(jnp.mean(resid_f * resid_f, 1, keepdims=True) + 1e-06)
    normed = (resid_f * inverse * norm_gain[None, :]).astype(jnp.bfloat16)
    expert_count = device_count // 2
    capacity = token_count * TOPK // expert_count + 1
    flat_ids = expert_ids.reshape(-1)
    onehot = (flat_ids[:, None] == jnp.arange(expert_count, dtype=jnp.int32)[None, :]).astype(
        jnp.int32
    )
    before = jnp.cumsum(onehot, 0) - onehot
    slot_in = jnp.sum(before * onehot, 1)
    target = flat_ids * capacity + slot_in
    token_of = jnp.arange(token_count * TOPK, dtype=jnp.int32) // TOPK
    slot_token = (
        jnp.full((expert_count * capacity,), token_count, jnp.int32).at[target].set(token_of)
    )
    normed_pad = jnp.concatenate([normed, jnp.zeros((1, D), jnp.bfloat16)], 0)
    packed = normed_pad[slot_token]
    outgoing = jnp.repeat(packed.reshape(expert_count, capacity, D), 2, axis=0)
    incoming = send_out(outgoing)
    expert_rows = incoming.reshape(device_count * capacity, D)
    gate_act = jnp.dot(expert_rows, w_gate[0], preferred_element_type=jnp.float32)
    up_act = jnp.dot(expert_rows, w_up[0], preferred_element_type=jnp.float32)
    inner = (jax.nn.silu(gate_act) * up_act).astype(jnp.bfloat16)
    part = jnp.dot(inner, w_down[0], preferred_element_type=jnp.float32).astype(jnp.bfloat16)
    returned = send_back(part.reshape(device_count, capacity, D))
    halves = returned.reshape(expert_count, 2, capacity, D).astype(jnp.float32)
    expert_out = (halves[:, 0] + halves[:, 1]).reshape(expert_count * capacity, D)
    picked = expert_out[target].reshape(token_count, TOPK, D)
    moe = jnp.sum(route_weights[:, :, None] * picked, 1)
    return (resid_f + moe).astype(jnp.bfloat16)


def solution(mesh):
    in_specs = (
        P(("ctx", "exp"), None),
        P(("ctx", "exp"), None),
        P(("ctx", "exp"), None),
        P(("ctx", "exp"), None),
        P(("ctx", "exp")),
        P(),
        P(("ctx", "exp"), None, None),
        P(("ctx", "exp"), None, None),
        P(("ctx", "exp"), None, None),
        P(("ctx", "exp"), None),
        P(("ctx", "exp"), None),
    )
    out_specs = P(("ctx", "exp"), None)
    return jax.shard_map(
        on_device, mesh=mesh, in_specs=in_specs, out_specs=out_specs, check_vma=False
    )
```

profile of v0, /device:TPU:0, one launch (start us, length us, event | category | flops | bytes accessed | tf_op | source)
XLA Modules:
  0.0 850.6 jit_solution(14954667422513652937)
XLA Ops:
  0.0 0.7 convert_bitcast_fusion
  0.7 5.0 collective-permute-start.3
  5.7 3.9 collective-permute-start.4
  9.6 2.9 collective-permute-start.5
  12.4 1.0 copy.20
  13.5 5.5 collective-permute-start.6
  19.0 2.8 collective-permute-start
  21.8 0.8 copy.31
  22.6 0.1 eq.49
  22.7 0.1 eq.45
  22.8 0.7 broadcast_multiply_fusion
  23.5 18.0 %reduce-window.6 = s32[64,8,128]{2,1,0:T(8,128)S(1)} reduce-window(s32[64,8,128]{2,1,0:T(8,128)S(1)} %fusion.27, s32[]{:T(128)} %constant.60.clone.1), window={size=1x1x128 pad=0_0x0_0x127_0}, to_apply=%region_3.4 | reduce-window | flops 8323072 | bytes 524292 | tf_op jit(solution)/shard_map/reduce-window
  41.6 0.1 slice.20
  41.7 0.1 copy.33
  41.9 0.1 copy.34
  42.0 0.1 broadcast_add_fusion
  42.1 0.1 copy.30
  42.2 0.1 mul.85
  42.3 0.1 fusion.26
  42.4 0.6 copy-done.4
  43.0 4.3 scatter_custom_fusion
  47.3 1.6 copy.24
  48.9 0.0 collective-permute-done.3
  48.9 3.9 collective-permute-start.7
  52.8 0.0 collective-permute-done.4
  52.8 3.2 collective-permute-start.8
  56.0 0.0 collective-permute-done.5
  56.0 4.5 collective-permute-start.1
  60.6 0.0 collective-permute-done
  60.6 2.0 collective-permute-start.2
  62.6 0.2 compare_and_fusion
  62.8 1.4 collective-permute-done.1
  64.2 1.4 collective-permute-done.2
  65.6 0.9 pad_maximum_fusion
  66.5 0.2 copy.19
  66.7 0.0 collective-permute-done.6
  66.7 0.0 collective-permute-done.7
  66.8 0.0 collective-permute-done.8
  66.8 0.1 pad_maximum_fusion.1
  66.8 4.5 fusion.36
  71.3 5.2 fusion.23
  76.6 1.8 copy.28
  78.4 0.4 fusion.18
  78.8 0.0 copy-start
  78.8 0.9 copy-done
  79.7 0.3 fusion.20
  80.0 0.1 concatenate.15
  80.0 7.4 gather_fusion
  87.4 10.2 %reshape.166 = bf16[64,17,3584]{2,1,0:T(8,128)(2,1)} reshape(bf16[1088,3584]{1,0:T(8,128)(2,1)} %gather_fusion) | data formatting | bytes 15597568 | tf_op jit(solution)/shard_map/reshape | solution.py:115
  97.6 8.5 broadcast_in_dim.25
  106.1 260.0 %all_to_all.10 = bf16[128,17,3584]{2,1,0:T(8,128)(2,1)} all-to-all(bf16[128,17,3584]{2,1,0:T(8,128)(2,1)S(1)} %bitcast.83), channel_id=1, replica_groups=mesh['ctx'=8,'exp'=16] {'ctx','exp'}, dimensions={0} | all-to-all | bytes 31195136 | tf_op jit(solution)/shard_map/all_to_all | solution.py:47
  366.1 20.1 %reshape.168 = bf16[2176,3584]{1,0:T(8,128)(2,1)} reshape(bf16[128,17,3584]{2,1,0:T(8,128)(2,1)} %all_to_all.10) | data formatting | bytes 31195136 | tf_op jit(solution)/shard_map/reshape | solution.py:117
  386.2 17.8 %fusion.9 = f32[2176,640]{1,0:T(8,128)} fusion(bf16[2176,3584]{1,0:T(8,128)(2,1)} %reshape.168, bf16[1,3584,640]{2,1,0:T(8,128)(2,1)} %param.17), kind=kOutput, calls=%fused_computation.19 | convolution fusion | flops 9982443520 | bytes 25755648 | tf_op jit(solution)/shard_map/dot_general | solution.py:118
  404.0 37.7 %convolution_convert_fusion = bf16[2176,3584]{1,0:T(8,128)(2,1)} fusion(bf16[1,640,3584]{2,1,0:T(8,128)(2,1)} %param.19, bf16[2176,3584]{1,0:T(8,128)(2,1)} %reshape.168, f32[2176,640]{1,0:T(8,128)} %fusion.9, bf16[1,3584,640]{2,1,0:T(8,128)(2,1)} %param.18), kind=kOutput, calls=%fused_computation.4 | convolution fusion | flops 19981041664 | bytes 45940736 | tf_op jit(solution)/shard_map/dot_general | solution.py:121
  441.6 19.4 %reshape.169 = bf16[128,17,3584]{2,1,0:T(8,128)(2,1)} reshape(bf16[2176,3584]{1,0:T(8,128)(2,1)} %convolution_convert_fusion) | data formatting | bytes 31195136 | tf_op jit(solution)/shard_map/reshape | solution.py:122
  461.1 9.5 %all-to-all-start.1 = ((bf16[128,17,3584]{2,1,0:T(8,128)(2,1)}), bf16[128,17,3584]{2,1,0:T(8,128)(2,1)}, u32[]{:S(2)}, u32[]{:S(2)}) async-start(bf16[128,17,3584]{2,1,0:T(8,128)(2,1)} %reshape.169), calls=%async_computation.1 | async-start | bytes 44040192 | tf_op jit(solution)/shard_map/all_to_all | solution.py:53
  470.6 0.1 copy.29
  470.7 287.7 %all-to-all-done.1 = bf16[128,17,3584]{2,1,0:T(8,128)(2,1)} async-done(((bf16[128,17,3584]{2,1,0:T(8,128)(2,1)}), bf16[128,17,3584]{2,1,0:T(8,128)(2,1)}, u32[]{:S(2)}, u32[]{:S(2)}) %all-to-all-start.1) | async-done | bytes 15597600 | tf_op jit(solution)/shard_map/all_to_all | solution.py:53
  758.4 23.9 %convert.4 = f32[64,2,17,3584]{3,2,1,0:T(8,128)} convert(bf16[64,2,17,3584]{3,2,1,0:T(8,128)(2,1)} %bitcast.20) | non-fusion elementwise | flops 7798784 | bytes 46792704 | tf_op jit(solution)/shard_map/convert_element_type | solution.py:123
  782.3 22.5 %fusion.1 = f32[64,1,17,3584]{3,2,0,1:T(8,128)} fusion(f32[64,2,17,3584]{3,2,1,0:T(8,128)} %convert.4), kind=kLoop, calls=%fused_computation.6 | loop fusion | flops 3899392 | bytes 46792704 | tf_op jit(solution)/shard_map/add | solution.py:124
  804.8 14.9 %add.101 = f32[1088,3584]{1,0:T(8,128)} reshape(f32[64,1,17,3584]{3,2,0,1:T(8,128)} %fusion.1) | data formatting | bytes 31195136 | tf_op jit(solution)/shard_map/add | solution.py:124
  819.7 19.0 %gather_fusion.1 = f32[1024,3584]{1,0:T(8,128)} fusion(f32[1088,3584]{1,0:T(8,128)} %add.101, s32[1024]{0:T(1024)S(1)} %broadcast_clamp_fusion), kind=kCustom, calls=%fused_computation.1 | custom fusion | bytes 29364224 | tf_op jit(solution)/shard_map/gather | solution.py:125
  838.8 10.8 %fusion.2 = f32[128,3584]{1,0:T(8,128)S(1)} fusion(f32[1024,3584]{1,0:T(8,128)} %gather_fusion.1, f32[128,8]{1,0:T(8,128)S(1)} %copy.29), kind=kLoop, calls=%fused_computation.9 | loop fusion | flops 6881280 | bytes 16519168 | tf_op jit(solution)/shard_map/reduce_sum | solution.py:126
  849.5 1.1 fusion.21
  (23 shorter events, 0.1 us)
Async XLA Ops:
  0.7 48.2 %collective-permute-start.3 = (bf16[128,1]{0,1:T(2,128)(2,1)S(1)}, bf16[128,1]{0,1:T(2,128)(2,1)S(1)}, u32[]{:S(2)}, u32[]{:S(2)}) collective-permute-start(bf16[128,1]{0,1:T(2,128)(2,1)S(1)} %get-tuple-element.7), channel_id=1, source_target_pairs={{0,3},{1,4},{2,5},{3,6},{4,7},{5,8},{6,9},{7,10},{8,11},{9,12},{10... | collective-permute-start | bytes 776 | tf_op jit(solution)/shard_map/ppermute | solution.py:20
  5.7 47.2 %collective-permute-start.4 = (bf16[128,1]{0,1:T(2,128)(2,1)S(1)}, bf16[128,1]{0,1:T(2,128)(2,1)S(1)}, u32[]{:S(2)}, u32[]{:S(2)}) collective-permute-start(bf16[128,1]{0,1:T(2,128)(2,1)S(1)} %get-tuple-element.7), channel_id=1, source_target_pairs={{0,2},{1,3},{2,4},{3,5},{4,6},{5,7},{6,8},{7,9},{8,10},{9,11},{10,... | collective-permute-start | bytes 776 | tf_op jit(solution)/shard_map/ppermute | solution.py:20
  9.6 46.5 %collective-permute-start.5 = (bf16[128,1]{0,1:T(2,128)(2,1)S(1)}, bf16[128,1]{0,1:T(2,128)(2,1)S(1)}, u32[]{:S(2)}, u32[]{:S(2)}) collective-permute-start(bf16[128,1]{0,1:T(2,128)(2,1)S(1)} %get-tuple-element.7), channel_id=1, source_target_pairs={{0,1},{1,2},{2,3},{3,4},{4,5},{5,6},{6,7},{7,8},{8,9},{9,10},{10,1... | collective-permute-start | bytes 776 | tf_op jit(solution)/shard_map/ppermute | solution.py:20
  13.5 53.3 %collective-permute-start.6 = (bf16[128,512]{0,1:T(8,128)(2,1)S(1)}, bf16[128,512]{0,1:T(8,128)(2,1)S(1)}, u32[]{:S(2)}, u32[]{:S(2)}) collective-permute-start(bf16[128,512]{0,1:T(8,128)(2,1)S(1)} %copy.20), channel_id=1, source_target_pairs={{0,3},{1,4},{2,5},{3,6},{4,7},{5,8},{6,9},{7,10},{8,11},{9,12},{10... | collective-permute-start | bytes 393224 | tf_op jit(solution)/shard_map/ppermute | solution.py:20
  19.0 41.6 %collective-permute-start = (bf16[128,512]{1,0:T(8,128)(2,1)}, bf16[128,512]{1,0:T(8,128)(2,1)S(1)}, u32[]{:S(2)}, u32[]{:S(2)}) collective-permute-start(bf16[128,512]{1,0:T(8,128)(2,1)} %param.14), channel_id=1, source_target_pairs={{0,3},{1,4},{2,5},{3,6},{4,7},{5,8},{6,9},{7,10},{8,11},{9,12},{10... | collective-permute-start | bytes 393224 | tf_op jit(solution)/shard_map/ppermute | solution.py:20
  42.4 0.6 copy-start.4
  48.9 17.8 %collective-permute-start.7 = (bf16[128,512]{0,1:T(8,128)(2,1)S(1)}, bf16[128,512]{0,1:T(8,128)(2,1)S(1)}, u32[]{:S(2)}, u32[]{:S(2)}) collective-permute-start(bf16[128,512]{0,1:T(8,128)(2,1)S(1)} %copy.20), channel_id=1, source_target_pairs={{0,2},{1,3},{2,4},{3,5},{4,6},{5,7},{6,8},{7,9},{8,10},{9,11},{10,... | collective-permute-start | bytes 393224 | tf_op jit(solution)/shard_map/ppermute | solution.py:20
  52.8 13.9 %collective-permute-start.8 = (bf16[128,512]{0,1:T(8,128)(2,1)S(1)}, bf16[128,512]{0,1:T(8,128)(2,1)S(1)}, u32[]{:S(2)}, u32[]{:S(2)}) collective-permute-start(bf16[128,512]{0,1:T(8,128)(2,1)S(1)} %copy.20), channel_id=1, source_target_pairs={{0,1},{1,2},{2,3},{3,4},{4,5},{5,6},{6,7},{7,8},{8,9},{9,10},{10,1... | collective-permute-start | bytes 393224 | tf_op jit(solution)/shard_map/ppermute | solution.py:20
  56.0 8.1 collective-permute-start.1
  60.6 5.0 collective-permute-start.2
  71.3 7.1 copy-start.2
  76.6 3.1 copy-start.3
  78.8 0.9 copy-start
  461.1 9.5 %copy-start.6 = (f32[128,8]{0,1:T(8,128)S(1)}, f32[128,8]{0,1:T(8,128)}, u32[]{:S(2)}) copy-start(f32[128,8]{0,1:T(8,128)} %param.21) | copy-start | bytes 12292
  461.1 9.6 %copy-start.5 = (s32[1024,1]{0,1:T(1,128)S(1)}, s32[1024,1]{0,1:T(1,128)}, u32[]{:S(2)}) copy-start(s32[1024,1]{0,1:T(1,128)} %copy-done.4) | copy-start | bytes 12292
  461.1 297.4 %all-to-all-start.1 = ((bf16[128,17,3584]{2,1,0:T(8,128)(2,1)}), bf16[128,17,3584]{2,1,0:T(8,128)(2,1)}, u32[]{:S(2)}, u32[]{:S(2)}) async-start(bf16[128,17,3584]{2,1,0:T(8,128)(2,1)} %reshape.169), calls=%async_computation.1 | async-start | bytes 44040192 | tf_op jit(solution)/shard_map/all_to_all | solution.py:53
  838.8 10.8 %copy-start.1 = (bf16[128,3584]{1,0:T(8,128)(2,1)S(1)}, bf16[128,3584]{1,0:T(8,128)(2,1)}, u32[]{:S(2)}) copy-start(bf16[128,3584]{1,0:T(8,128)(2,1)} %copy-done) | copy-start | bytes 2752516
where the time goes:
time: 861 us; the launch traced here: 851 us
  waiting for transfers between devices  291 us (34%)
  blocking collectives  260 us (30%)
  local copies, waits for them, and re-layouts  112 us (13%)
  other arithmetic  79.7 us (9%)
  matrix products  65.1 us (8%)
  starting transfers between devices  43.2 us (5%)
    all_to_all x1, waiting for transfers between devices, send_back(): lax.all_to_all(buffer, ('ctx', 'exp'), split_axis=0, concat_axis=0, tiled...  288 us
    all_to_all x1, blocking collectives, send_out(): lax.all_to_all(buffer, ('ctx', 'exp'), split_axis=0, concat_axis=0, tiled...  260 us
    dot_general x1, matrix products, on_device(): jnp.dot(inner, w_down[0], preferred_element_type=jnp.float32)  37.7 us
    ppermute x9, starting transfers between devices, from_behind(): lax.ppermute(value, axis, [(source, source + steps) for source in range(i...  33.7 us
    convert_element_type x1, other arithmetic, on_device(): halves = returned.reshape(expert_count, 2, capacity, D).astype(jnp.float32)  23.9 us
    add x1, other arithmetic, on_device(): halves[:, 0] + halves[:, 1]  22.5 us
    reshape x1, local copies, waits for them, and re-layouts, on_device(): expert_rows = incoming.reshape(device_count * capacity, D)  20.1 us
    reshape x1, local copies, waits for them, and re-layouts, on_device(): returned = send_back(part.reshape(device_count, capacity, D))  19.4 us
  transfers between devices with their start and end apart: 10, of which 3 were waited for; matrix products, arithmetic and copies ran while one was open for 3% of the time, Pallas kernels for 0%

commit v1 on v0

v1 whole, which is shorter than its diff:
```python
import jax
import jax.numpy as jnp
from jax import lax
from jax.experimental import pallas as pl
from jax.experimental.pallas import tpu as pltpu
from jax.sharding import PartitionSpec as P

D = 3584
KV_HEADS = 4
HEAD_DIM = 128
TOPK = 8
WINDOW = 4
GROUP = 7
TOK = 128
CAP = 17
FF_HALF = 640
NQ = 7
CW = D // NQ
HW = CW // 2
SLAB = 144
NB = 2

MESH = pl.DeviceIdType.MESH
masked_score = -1e30
bf16 = jnp.bfloat16
f32 = jnp.float32


def coords():
    ctx, ex = lax.axis_index("ctx"), lax.axis_index("exp")
    return ctx // 2, ctx % 2, ex // 4, ex % 4


def place(x, c, z, y):
    return (x * 2 + c, z * 4 + y)


def greet(partners):
    barrier = pltpu.get_barrier_semaphore()
    for partner in partners:
        pl.semaphore_signal(barrier, inc=1, device_id=partner, device_id_type=MESH)
    pl.semaphore_wait(barrier, len(partners))


def remote(src, dst, send_sem, recv_sem, device):
    return pltpu.make_async_remote_copy(
        src_ref=src,
        dst_ref=dst,
        send_sem=send_sem,
        recv_sem=recv_sem,
        device_id=device,
        device_id_type=MESH,
    )


def plus(value, steps):
    return lax.rem(value + steps, 4)


def attend_kernel(
    hid, q, k, v, doc_row, doc_col, meta, gain,
    resid_out, nrm_out, meta_out,
    kw, vw, docw, halo_ss, halo_rs, meta_ss, meta_rs,
):
    x, c, z, y = coords()
    rank = lax.axis_index("ctx") * 16 + lax.axis_index("exp")

    def by_rank(steps):
        other = lax.rem(rank + steps + 128, 128)
        return (other // 16, lax.rem(other, 16))

    group = [(dc, dy) for dc in range(2) for dy in range(4) if (dc, dy) != (0, 0)]
    peers = [place(x, lax.rem(c + dc, 2), z, plus(y, dy)) for dc, dy in group]
    greet([by_rank(s) for s in (1, 2, 3, -1, -2, -3)] + peers)
    mine = c * 4 + y
    copies = []
    for d in range(1, WINDOW):
        for i, (src, dst) in enumerate(((k, kw), (v, vw), (doc_row, docw))):
            copies.append(
                remote(src, dst.at[WINDOW - 1 - d], halo_ss.at[d - 1, i], halo_rs.at[d - 1, i], by_rank(d))
            )
    halo = len(copies)
    for i, peer in enumerate(peers):
        copies.append(remote(meta, meta_out.at[mine], meta_ss.at[i], meta_rs.at[i], peer))
    for copy in copies:
        copy.start()
    meta_out[mine] = meta[...]
    kw[WINDOW - 1] = k[...]
    vw[WINDOW - 1] = v[...]
    docw[WINDOW - 1] = doc_row[...]
    for copy in copies[:halo]:
        copy.wait_recv()

    key_doc = jnp.concatenate([docw[i][0:1, :] for i in range(WINDOW)], 1)
    span = WINDOW * TOK
    key_pos = lax.broadcasted_iota(jnp.int32, (TOK, span), 1) + (rank - (WINDOW - 1)) * TOK
    query_pos = lax.broadcasted_iota(jnp.int32, (TOK, span), 0) + rank * TOK
    visible = (doc_col[...] == key_doc) & (key_pos <= query_pos) & (key_pos >= 0)
    square = jnp.zeros((TOK, 1), f32)
    for g in range(KV_HEADS):
        cols = slice(g * HEAD_DIM, (g + 1) * HEAD_DIM)
        keys = kw[:, :, cols].reshape(span, HEAD_DIM)
        values = vw[:, :, cols].reshape(span, HEAD_DIM)
        for h in range(GROUP):
            at = (g * GROUP + h) * HEAD_DIM
            here = slice(at, at + HEAD_DIM)
            scores = lax.dot_general(
                q[:, here], keys, (((1,), (1,)), ((), ())), preferred_element_type=f32
            ) * (HEAD_DIM ** -0.5)
            scores = jnp.where(visible, scores, masked_score)
            exps = jnp.exp(scores - jnp.max(scores, 1, keepdims=True))
            probs = (exps / jnp.sum(exps, 1, keepdims=True)).astype(bf16)
            context = jnp.dot(probs, values, preferred_element_type=f32).astype(bf16)
            resid = (hid[:, here].astype(f32) + context.astype(f32)).astype(bf16)
            resid_out[:, here] = resid
            resid_f = resid.astype(f32)
            square += jnp.sum(resid_f * resid_f, 1, keepdims=True)
    inverse = lax.rsqrt(square * (1.0 / D) + 1e-06)
    for n in range(NQ):
        cols = slice(n * CW, (n + 1) * CW)
        nrm_out[n] = (resid_out[:, cols].astype(f32) * inverse * gain[:, cols]).astype(bf16)
    for copy in copies[halo:]:
        copy.wait_recv()
    for copy in copies:
        copy.wait_send()


def find_slots(meta, slots, weights, c, y):
    s = lax.broadcasted_iota(jnp.int32, (16, TOPK, TOK), 0)
    expert = (((s >> 2) * 2 + c) * 8 + (s & 3) * 2 + (y >> 1)).astype(f32)
    earlier = lax.broadcasted_iota(jnp.int32, (TOK, TOK), 0) < lax.broadcasted_iota(
        jnp.int32, (TOK, TOK), 1
    )
    earlier = jnp.where(earlier, 1.0, 0.0).astype(bf16)
    for b in range(8):
        ids = meta[b][0:TOPK, :]
        hit = ids[None] == expert
        member = jnp.sum(jnp.where(hit, 1.0, 0.0), 1)
        before = jnp.dot(member.astype(bf16), earlier, preferred_element_type=f32)
        slots[:, b, :] = jnp.where(member > 0.5, before + float(CAP * b), -1.0)
        if weights is not None:
            weights[:, b, :] = jnp.sum(jnp.where(hit, meta[b][TOPK:, :][None], 0.0), 1)


def fill_places(slots, weights, out):
    def one(s, carry):
        rows = lax.broadcasted_iota(jnp.int32, (SLAB, TOK), 0).astype(f32)
        slot = slots[s]
        weight = None if weights is None else weights[s]
        for b in range(8):
            value = 1.0 if weight is None else weight[b : b + 1, :]
            out[s, :, b * TOK : (b + 1) * TOK] = jnp.where(
                rows == slot[b : b + 1, :], value, 0.0
            ).astype(bf16)
        return carry

    lax.fori_loop(0, 16, one, 0)


def expert_kernel(
    nrm, meta, wg_hbm, wu_hbm,
    inner_out, ma, mb, xa, xb,
    tok, places, slots, sa, sb, gate, up, wg, wu, xv,
    ay_ss, ay_rs, ac_ss, ac_rs, p1_ss, p1_rs, p2_ss, p2_rs, loc, wsem, lsem,
):
    x, c, z, y = coords()
    core = place(x, 1 - c, z, y)
    ypeer = [place(x, c, z, plus(y, d)) for d in range(1, 4)]
    xpeer = [place(plus(x, d), c, z, y) for d in range(1, 4)]
    zpeer = [place(x, c, plus(z, d), y) for d in range(1, 4)]
    greet([core] + ypeer + xpeer + zpeer)
    mine = c * 4 + y

    def ay(n, d):
        return remote(nrm.at[n], tok.at[n, mine], ay_ss.at[n, d - 1], ay_rs.at[n, d - 1], ypeer[d - 1])

    def ac(n, d):
        if d == 0:
            src = nrm.at[n]
            at = mine
        else:
            at = c * 4 + plus(y, 4 - d)
            src = tok.at[n, at]
        return remote(src, tok.at[n, at], ac_ss.at[n, d], ac_rs.at[n, d], core)

    def p1(n, buf, d):
        xp, zp = plus(x, d), plus(z, d)
        return (
            remote(sa.at[buf, xp], ma.at[n, :, x], p1_ss.at[n, 0, d - 1], p1_rs.at[n, 0, d - 1], xpeer[d - 1]),
            remote(sb.at[buf, zp], mb.at[n, :, z], p1_ss.at[n, 1, d - 1], p1_rs.at[n, 1, d - 1], zpeer[d - 1]),
        )

    def own(n, buf):
        return (
            pltpu.make_async_copy(sa.at[buf, x], ma.at[n, :, x], loc.at[n, 0]),
            pltpu.make_async_copy(sb.at[buf, z], mb.at[n, :, z], loc.at[n, 1]),
        )

    def p2(n, d):
        xp, zp = plus(x, d), plus(z, d)
        return (
            remote(ma.at[n, zp], xa.at[n, z], p2_ss.at[n, 0, d - 1], p2_rs.at[n, 0, d - 1], zpeer[d - 1]),
            remote(mb.at[n, xp], xb.at[n, x], p2_ss.at[n, 1, d - 1], p2_rs.at[n, 1, d - 1], xpeer[d - 1]),
        )

    weights = [
        pltpu.make_async_copy(wg_hbm, wg, wsem.at[0]),
        pltpu.make_async_copy(wu_hbm, wu, wsem.at[1]),
    ]
    for copy in weights:
        copy.start()

    def start_gather(n, carry):
        for d in range(1, 4):
            ay(n, d).start()
        ac(n, 0).start()
        tok[n, mine] = nrm[n]
        return carry

    lax.fori_loop(0, NQ, start_gather, 0)

    def forward(n):
        for d in range(1, 4):
            ay(n, d).wait_recv()
            ac(n, d).start()

    find_slots(meta, slots, None, c, y)
    fill_places(slots, None, places)
    forward(0)
    gate[...] = jnp.zeros_like(gate)
    up[...] = jnp.zeros_like(up)
    for copy in weights:
        copy.wait()

    def step(n, carry):
        @pl.when(n < NQ)
        def _():
            for d in range(4):
                ac(n, d).wait_recv()
            buf = lax.rem(n, NB)

            @pl.when(n >= NB)
            def _():
                for d in range(1, 4):
                    for copy in p1(n - NB, buf, d):
                        copy.wait_send()

            chunk = tok[n].reshape(8 * TOK, CW)
            for xp in range(4):
                rows = places[xp * 4 : xp * 4 + 4].reshape(4 * SLAB, 8 * TOK)
                packed = jnp.dot(rows, chunk, preferred_element_type=f32).astype(bf16)
                packed = packed.reshape(4, SLAB, CW)
                sa[buf, xp] = packed[:, :, :HW]
                sb[buf, :, xp] = packed[:, :, HW:]
            for d in range(1, 4):
                for copy in p1(n, buf, d):
                    copy.start()
            for copy in own(n, buf):
                copy.start()

            @pl.when(n + 1 < NQ)
            def _():
                forward(n + 1)

        @pl.when((n >= 1) & (n <= NQ))
        def _():
            for d in range(1, 4):
                for copy in p1(n - 1, 0, d):
                    copy.wait_recv()
            for copy in own(n - 1, 0):
                copy.wait()
            for d in range(1, 4):
                for copy in p2(n - 1, d):
                    copy.start()

        @pl.when(n >= 2)
        def _():
            m = n - 2
            loads = [
                pltpu.make_async_copy(ma.at[m, z], xv.at[z, :, :, 0:HW], lsem.at[0]),
                pltpu.make_async_copy(mb.at[m, x], xv.at[:, x, :, HW:CW], lsem.at[1]),
            ]
            for load in loads:
                load.start()
            for d in range(1, 4):
                for copy in p2(m, d):
                    copy.wait_recv()
                zs, xs = plus(z, 4 - d), plus(x, 4 - d)
                more = [
                    pltpu.make_async_copy(xa.at[m, zs], xv.at[zs, :, :, 0:HW], lsem.at[2 * d]),
                    pltpu.make_async_copy(xb.at[m, xs], xv.at[:, xs, :, HW:CW], lsem.at[2 * d + 1]),
                ]
                for load in more:
                    load.start()
                loads += more
            for load in loads:
                load.wait()
            for i in range(4):
                rows = xv[i].reshape(4 * SLAB, CW)
                gate[i] += jnp.dot(rows, wg[m], preferred_element_type=f32)
                up[i] += jnp.dot(rows, wu[m], preferred_element_type=f32)

        return carry

    lax.fori_loop(0, NQ + 2, step, 0)
    for i in range(4):
        value = gate[i]
        inner_out[i] = (value / (1.0 + jnp.exp(-value)) * up[i]).astype(bf16)

    def finish(n, carry):
        for d in range(1, 4):
            ay(n, d).wait_send()
            for copy in p2(n, d):
                copy.wait_send()
        for d in range(4):
            ac(n, d).wait_send()
        return carry

    lax.fori_loop(0, NQ, finish, 0)
    for n in range(NQ - NB, NQ):
        for d in range(1, 4):
            for copy in p1(n, n % NB, d):
                copy.wait_send()


def return_kernel(
    inner, meta, resid, wd_hbm,
    out, ra, rb, ya, yb,
    places, slots, weights, sr, wd, rv, total, half, core_in, mix, y_in,
    p1_ss, p1_rs, p2_ss, p2_rs, rc_ss, rc_rs, ry_ss, ry_rs, loc, wsem, lsem,
):
    x, c, z, y = coords()
    core = place(x, 1 - c, z, y)
    ypeer = [place(x, c, z, plus(y, d)) for d in range(1, 4)]
    xpeer = [place(plus(x, d), c, z, y) for d in range(1, 4)]
    zpeer = [place(x, c, plus(z, d), y) for d in range(1, 4)]
    load_wd = pltpu.make_async_copy(wd_hbm, wd, wsem)
    load_wd.start()
    greet([core] + ypeer + xpeer + zpeer)

    def p1(n, buf, d):
        xp, zp = plus(x, d), plus(z, d)
        return (
            remote(sr.at[buf, zp, :, :, 0:HW], ra.at[n, :, z], p1_ss.at[n, 0, d - 1], p1_rs.at[n, 0, d - 1], zpeer[d - 1]),
            remote(sr.at[buf, :, xp, :, HW:CW], rb.at[n, :, x], p1_ss.at[n, 1, d - 1], p1_rs.at[n, 1, d - 1], xpeer[d - 1]),
        )

    def own(n, buf):
        return (
            pltpu.make_async_copy(sr.at[buf, z, :, :, 0:HW], ra.at[n, :, z], loc.at[n, 0]),
            pltpu.make_async_copy(sr.at[buf, :, x, :, HW:CW], rb.at[n, :, x], loc.at[n, 1]),
        )

    def p2(n, d):
        xp, zp = plus(x, d), plus(z, d)
        return (
            remote(ra.at[n, xp], ya.at[n, x], p2_ss.at[n, 0, d - 1], p2_rs.at[n, 0, d - 1], xpeer[d - 1]),
            remote(rb.at[n, zp], yb.at[n, z], p2_ss.at[n, 1, d - 1], p2_rs.at[n, 1, d - 1], zpeer[d - 1]),
        )

    def rc(n):
        return remote(
            half.at[lax.rem(n, 2), 1 - c], core_in.at[n], rc_ss.at[n], rc_rs.at[n], core
        )

    def ry(n, d):
        return remote(
            mix.at[lax.rem(n, 2), plus(y, d)], y_in.at[n, d - 1], ry_ss.at[n, d - 1], ry_rs.at[n, d - 1], ypeer[d - 1]
        )

    load_wd.wait()

    def step(n, carry):
        @pl.when(n < NQ)
        def _():
            buf = lax.rem(n, NB)

            @pl.when(n >= NB)
            def _():
                for d in range(1, 4):
                    for copy in p1(n - NB, buf, d):
                        copy.wait_send()

            down = wd[:, pl.ds(pl.multiple_of(n * CW, CW), CW)]
            for i in range(4):
                part = jnp.dot(inner[i], down, preferred_element_type=f32).astype(bf16)
                sr[buf, i] = part.reshape(4, SLAB, CW)
            for d in range(1, 4):
                for copy in p1(n, buf, d):
                    copy.start()
            for copy in own(n, buf):
                copy.start()

        @pl.when(n == 0)
        def _():
            find_slots(meta, slots, weights, c, y)
            fill_places(slots, weights, places)

        @pl.when((n >= 1) & (n <= NQ))
        def _():
            for d in range(1, 4):
                for copy in p1(n - 1, 0, d):
                    copy.wait_recv()
            for copy in own(n - 1, 0):
                copy.wait()
            for d in range(1, 4):
                for copy in p2(n - 1, d):
                    copy.start()

        @pl.when((n >= 2) & (n <= NQ + 1))
        def _():
            m = n - 2
            loads = [
                pltpu.make_async_copy(ra.at[m, x], rv.at[x, :, :, 0:HW], lsem.at[0]),
                pltpu.make_async_copy(rb.at[m, z], rv.at[:, z, :, HW:CW], lsem.at[1]),
            ]
            for load in loads:
                load.start()
            for d in range(1, 4):
                for copy in p2(m, d):
                    copy.wait_recv()
                zs, xs = plus(z, 4 - d), plus(x, 4 - d)
                more = [
                    pltpu.make_async_copy(ya.at[m, xs], rv.at[xs, :, :, 0:HW], lsem.at[2 * d]),
                    pltpu.make_async_copy(yb.at[m, zs], rv.at[:, zs, :, HW:CW], lsem.at[2 * d + 1]),
                ]
                for load in more:
                    load.start()
                loads += more
            for load in loads:
                load.wait()
            moe = lax.dot_general(
                places[...].reshape(16 * SLAB, 8 * TOK),
                rv[...].reshape(16 * SLAB, CW),
                (((0,), (0,)), ((), ())),
                preferred_element_type=f32,
            )
            total[lax.rem(m, 2)] = moe.reshape(2, 4, TOK, CW)

            @pl.when(m >= 2)
            def _():
                rc(m - 2).wait_send()

            half[lax.rem(m, 2)] = total[lax.rem(m, 2)].astype(bf16)
            rc(m).start()

        @pl.when((n >= 3) & (n <= NQ + 2))
        def _():
            m = n - 3
            rc(m).wait_recv()

            @pl.when(m >= 2)
            def _():
                for d in range(1, 4):
                    ry(m - 2, d).wait_send()

            mix[lax.rem(m, 2)] = (total[lax.rem(m, 2), c] + core_in[m].astype(f32)).astype(bf16)
            for d in range(1, 4):
                ry(m, d).start()

        @pl.when(n >= 4)
        def _():
            m = n - 4
            value = mix[lax.rem(m, 2), y].astype(f32)
            for d in range(1, 4):
                ry(m, d).wait_recv()
                value += y_in[m, d - 1].astype(f32)
            cols = pl.ds(pl.multiple_of(m * CW, CW), CW)
            out[:, cols] = (resid[:, cols].astype(f32) + value).astype(bf16)

        return carry

    lax.fori_loop(0, NQ + 4, step, 0)

    def finish(n, carry):
        for d in range(1, 4):
            for copy in p2(n, d):
                copy.wait_send()
        return carry

    lax.fori_loop(0, NQ, finish, 0)
    for n in range(NQ - NB, NQ):
        for d in range(1, 4):
            for copy in p1(n, n % NB, d):
                copy.wait_send()
    for n in range(NQ - 2, NQ):
        rc(n).wait_send()
        for d in range(1, 4):
            ry(n, d).wait_send()


VM = pl.BlockSpec(memory_space=pltpu.VMEM)
ANY = pl.BlockSpec(memory_space=pl.ANY)


def dma(*shape):
    return pltpu.SemaphoreType.DMA(shape)


def params(collective_id):
    return pltpu.CompilerParams(
        collective_id=collective_id, has_side_effects=True, vmem_limit_bytes=62 << 20
    )


def on_device(
    hidden_in, queries, key_rows, value_rows, document_ids, norm_gain,
    w_gate, w_up, w_down, expert_ids, route_weights,
):
    docs = document_ids.astype(f32)
    doc_row = jnp.broadcast_to(docs[None, :], (8, TOK))
    meta = jnp.concatenate([expert_ids.T.astype(f32), route_weights.T], 0)
    resid, nrm, meta_all = pl.pallas_call(
        attend_kernel,
        out_shape=(
            jax.ShapeDtypeStruct((TOK, D), bf16),
            jax.ShapeDtypeStruct((NQ, TOK, CW), bf16),
            jax.ShapeDtypeStruct((8, 2 * TOPK, TOK), f32),
        ),
        in_specs=[VM] * 8,
        out_specs=(VM, VM, VM),
        scratch_shapes=[
            pltpu.VMEM((WINDOW, TOK, KV_HEADS * HEAD_DIM), bf16),
            pltpu.VMEM((WINDOW, TOK, KV_HEADS * HEAD_DIM), bf16),
            pltpu.VMEM((WINDOW, 8, TOK), f32),
            dma(3, 3), dma(3, 3), dma(7), dma(7),
        ],
        compiler_params=params(0),
    )(hidden_in, queries, key_rows, value_rows, doc_row, docs[:, None], meta, norm_gain[None, :])

    landing = jax.ShapeDtypeStruct((NQ, 4, 4, SLAB, HW), bf16)
    inner, *_ = pl.pallas_call(
        expert_kernel,
        out_shape=(jax.ShapeDtypeStruct((4, 4 * SLAB, FF_HALF), bf16),) + (landing,) * 4,
        in_specs=[VM, VM, ANY, ANY],
        out_specs=(VM,) + (ANY,) * 4,
        scratch_shapes=[
            pltpu.VMEM((NQ, 8, TOK, CW), bf16),
            pltpu.VMEM((16, SLAB, 8 * TOK), bf16),
            pltpu.VMEM((16, 8, TOK), f32),
            pltpu.VMEM((NB, 4, 4, SLAB, HW), bf16),
            pltpu.VMEM((NB, 4, 4, SLAB, HW), bf16),
            pltpu.VMEM((4, 4 * SLAB, FF_HALF), f32),
            pltpu.VMEM((4, 4 * SLAB, FF_HALF), f32),
            pltpu.VMEM((NQ, CW, FF_HALF), bf16),
            pltpu.VMEM((NQ, CW, FF_HALF), bf16),
            pltpu.VMEM((4, 4, SLAB, CW), bf16),
            dma(NQ, 3), dma(NQ, 3), dma(NQ, 4), dma(NQ, 4),
            dma(NQ, 2, 3), dma(NQ, 2, 3), dma(NQ, 2, 3), dma(NQ, 2, 3),
            dma(NQ, 2), dma(2), dma(8),
        ],
        compiler_params=params(1),
    )(nrm, meta_all, w_gate.reshape(NQ, CW, FF_HALF), w_up.reshape(NQ, CW, FF_HALF))

    out, *_ = pl.pallas_call(
        return_kernel,
        out_shape=(jax.ShapeDtypeStruct((TOK, D), bf16),) + (landing,) * 4,
        in_specs=[VM, VM, VM, ANY],
        out_specs=(VM,) + (ANY,) * 4,
        scratch_shapes=[
            pltpu.VMEM((16, SLAB, 8 * TOK), bf16),
            pltpu.VMEM((16, 8, TOK), f32),
            pltpu.VMEM((16, 8, TOK), f32),
            pltpu.VMEM((NB, 4, 4, SLAB, CW), bf16),
            pltpu.VMEM((FF_HALF, D), bf16),
            pltpu.VMEM((4, 4, SLAB, CW), bf16),
            pltpu.VMEM((2, 2, 4, TOK, CW), f32),
            pltpu.VMEM((2, 2, 4, TOK, CW), bf16),
            pltpu.VMEM((NQ, 4, TOK, CW), bf16),
            pltpu.VMEM((2, 4, TOK, CW), bf16),
            pltpu.VMEM((NQ, 3, TOK, CW), bf16),
            dma(NQ, 2, 3), dma(NQ, 2, 3), dma(NQ, 2, 3), dma(NQ, 2, 3),
            dma(NQ), dma(NQ), dma(NQ, 3), dma(NQ, 3),
            dma(NQ, 2), pltpu.SemaphoreType.DMA, dma(8),
        ],
        compiler_params=params(2),
    )(inner, meta_all, resid, w_down.reshape(FF_HALF, D))
    return out


def solution(mesh):
    rows = P(("ctx", "exp"), None)
    whole = P(("ctx", "exp"), None, None)
    in_specs = (
        rows, rows, rows, rows, P(("ctx", "exp")), P(), whole, whole, whole, rows, rows,
    )
    return jax.shard_map(
        on_device, mesh=mesh, in_specs=in_specs, out_specs=rows, check_vma=False
    )
```

time: 861 us -> 463 us (0.54); the launches traced: 851 us -> 462 us
  Pallas kernels: 0 us -> 455 us
  waiting for transfers between devices: 291 us -> 0 us
  blocking collectives: 260 us -> 0 us
  local copies, waits for them, and re-layouts: 112 us -> 4.82 us
  other arithmetic: 79.7 us -> 2.63 us
  matrix products: 65.1 us -> 0 us
  starting transfers between devices: 43.2 us -> 0 us
    pallas_call x0 -> x3, Pallas kernels: none -> 455 us  [the longest x1 212 us: on_device(): pl.pallas_call(expert_kernel, out_shape=(jax.ShapeDtypeStruct((4, 4 * SLA...]
    all_to_all x1 -> x0, waiting for transfers between devices: 288 us -> none  [send_back(): lax.all_to_all(buffer, ('ctx', 'exp'), split_axis=0, concat_axis=0, tiled...]
    all_to_all x1 -> x0, blocking collectives: 260 us -> none  [send_out(): lax.all_to_all(buffer, ('ctx', 'exp'), split_axis=0, concat_axis=0, tiled...]
    dot_general x3 -> x0, matrix products: 60.6 us -> none  [the longest x1 37.7 us: on_device(): jnp.dot(inner, w_down[0], preferred_element_type=jnp.float32)]
    reshape x3 -> x0, local copies, waits for them, and re-layouts: 49.7 us -> none  [the longest x1 20.1 us: on_device(): expert_rows = incoming.reshape(device_count * capacity, D)]
    ppermute x9 -> x0, starting transfers between devices: 33.7 us -> none  [from_behind(): lax.ppermute(value, axis, [(source, source + steps) for source in range(i...]
    gather x2 -> x0, local copies, waits for them, and re-layouts: 26.4 us -> none  [the longest x1 19 us: on_device(): picked = expert_out[target].reshape(token_count, TOPK, D)]
    convert_element_type x5 -> x1, other arithmetic: 25.2 us -> 0.69 us  [on_device(): meta = jnp.concatenate([expert_ids.T.astype(f32), route_weights.T], 0)]
  transfers between devices with their start and end apart: 10 -> 0, of which waited for: 3 -> 0; matrix products, arithmetic and copies ran while one was open for 3% -> 0% of each run, Pallas kernels for 0% -> 0%
where the time goes in v1:
time: 463 us; the launch traced here: 462 us
  Pallas kernels  455 us (98%)
  local copies, waits for them, and re-layouts  4.82 us (1%)
    pallas_call x1, Pallas kernels, on_device(): pl.pallas_call(expert_kernel, out_shape=(jax.ShapeDtypeStruct((4, 4 * SLA...  212 us
    pallas_call x1, Pallas kernels, on_device(): pl.pallas_call(return_kernel, out_shape=(jax.ShapeDtypeStruct((TOK, D), b...  210 us
    pallas_call x1, Pallas kernels, on_device(): pl.pallas_call(attend_kernel, out_shape=(jax.ShapeDtypeStruct((TOK, D), b...  33 us

profile of v1, /device:TPU:0, one launch (start us, length us, event | category | flops | bytes accessed | tf_op | source)
XLA Modules:
  0.0 462.5 jit_solution(1513703552862889975)
XLA Ops:
  0.0 0.7 convert_bitcast_fusion.1
  0.7 0.6 broadcast_in_dim.12.doc_row
  1.3 0.7 convert_bitcast_fusion
  1.9 1.3 pad_maximum_fusion.meta
  3.2 1.3 broadcast_in_dim.14.gain
  4.6 0.7 copy.12.doc_col
  5.3 33.0 %shard_map.109 = (bf16[128,3584]{1,0:T(8,128)(2,1)}, bf16[7,128,512]{2,1,0:T(8,128)(2,1)}, f32[8,16,128]{2,1,0:T(8,128)}) custom-call(bf16[128,3584]{1,0:T(8,128)(2,1)} %hid.1, bf16[128,3584]{1,0:T(8,128)(2,1)} %q.1, bf16[128,512]{1,0:T(8,128)(2,1)} %k.1, bf16[128,512]{1,0:T(8,128)(2,1)} %v.1, f32[8,128]{1,0:T(8,128)} %broadcast_in_dim.12.doc_row, ...), custom_call_target="tpu_custom_call" | custom-call | tf_op jit(solution)/shard_map/pallas_call | solution.py:513
  38.3 212.4 %shard_map.110 = (bf16[4,576,640]{2,1,0:T(8,128)(2,1)}, bf16[7,4,4,144,256]{4,3,2,1,0:T(8,128)(2,1)}, bf16[7,4,4,144,256]{4,3,2,1,0:T(8,128)(2,1)}, bf16[7,4,4,1...) custom-call(bf16[7,128,512]{2,1,0:T(8,128)(2,1)} %get-tuple-element.10.nrm, f32[8,16,128]{2,1,0:T(8,128)} %get-tuple-element.11.meta, ...), custom_call_target="tpu_custom_call" | custom-call | tf_op jit(solution)/shard_map/pallas_call | solution.py:532
  250.7 209.6 %shard_map.111 = (bf16[128,3584]{1,0:T(8,128)(2,1)}, bf16[7,4,4,144,256]{4,3,2,1,0:T(8,128)(2,1)}, bf16[7,4,4,144,256]{4,3,2,1,0:T(8,128)(2,1)}, bf16[7,4,4,144,...) custom-call(bf16[4,576,640]{2,1,0:T(8,128)(2,1)} %get-tuple-element.12.inner, f32[8,16,128]{2,1,0:T(8,128)} %get-tuple-element.11.meta, ...), custom_call_target="tpu_custom_call" | custom-call | tf_op jit(solution)/shard_map/pallas_call | solution.py:555
  460.3 2.2 copy.14

commit v2 on v1

--- a/solution.py
+++ b/solution.py
@@ -19,6 +19,8 @@
 HW = CW // 2
 SLAB = 144
 NB = 2
+NF = 2
+NS = NQ - NF
 
 MESH = pl.DeviceIdType.MESH
 masked_score = -1e30
@@ -51,6 +53,10 @@
         device_id=device,
         device_id_type=MESH,
     )
+
+
+def fetched(n, parity):
+    return jnp.where(n < NF, 2 * n + parity, n + NF)
 
 
 def plus(value, steps):
@@ -159,9 +165,9 @@
 
 def expert_kernel(
     nrm, meta, wg_hbm, wu_hbm,
-    inner_out, ma, mb, xa, xb,
+    inner_out, ma, mb, xa, xb, pa, pb,
     tok, places, slots, sa, sb, gate, up, wg, wu, xv,
-    ay_ss, ay_rs, ac_ss, ac_rs, p1_ss, p1_rs, p2_ss, p2_rs, loc, wsem, lsem,
+    ay_ss, ay_rs, ac_ss, ac_rs, p1_ss, p1_rs, p2_ss, p2_rs, sw_ss, sw_rs, loc, wsem, lsem,
 ):
     x, c, z, y = coords()
     core = place(x, 1 - c, z, y)
@@ -170,13 +176,16 @@
     zpeer = [place(x, c, plus(z, d), y) for d in range(1, 4)]
     greet([core] + ypeer + xpeer + zpeer)
     mine = c * 4 + y
+    parity = lax.rem(y, 2)
+    pair = place(x, c, z, y + 1 - 2 * parity)
 
     def ay(n, d):
-        return remote(nrm.at[n], tok.at[n, mine], ay_ss.at[n, d - 1], ay_rs.at[n, d - 1], ypeer[d - 1])
+        src = nrm.at[fetched(n, lax.rem(y + d, 2))]
+        return remote(src, tok.at[n, mine], ay_ss.at[n, d - 1], ay_rs.at[n, d - 1], ypeer[d - 1])
 
     def ac(n, d):
         if d == 0:
-            src = nrm.at[n]
+            src = nrm.at[fetched(n, parity)]
             at = mine
         else:
             at = c * 4 + plus(y, 4 - d)
@@ -201,6 +210,14 @@
         return (
             remote(ma.at[n, zp], xa.at[n, z], p2_ss.at[n, 0, d - 1], p2_rs.at[n, 0, d - 1], zpeer[d - 1]),
             remote(mb.at[n, xp], xb.at[n, x], p2_ss.at[n, 1, d - 1], p2_rs.at[n, 1, d - 1], xpeer[d - 1]),
+        )
+
+    def swap(n, d):
+        zs, xs = plus(z, 4 - d), plus(x, 4 - d)
+        a, b = (ma.at[n, z], mb.at[n, x]) if d == 0 else (xa.at[n, zs], xb.at[n, xs])
+        return (
+            remote(a, pa.at[n, zs], sw_ss.at[n, 0, d], sw_rs.at[n, 0, d], pair),
+            remote(b, pb.at[n, xs], sw_ss.at[n, 1, d], sw_rs.at[n, 1, d], pair),
         )
 
     weights = [
@@ -214,10 +231,10 @@
         for d in range(1, 4):
             ay(n, d).start()
         ac(n, 0).start()
-        tok[n, mine] = nrm[n]
+        tok[n, mine] = nrm[fetched(n, parity)]
         return carry
 
-    lax.fori_loop(0, NQ, start_gather, 0)
+    lax.fori_loop(0, NS, start_gather, 0)
 
     def forward(n):
         for d in range(1, 4):
@@ -233,7 +250,7 @@
         copy.wait()
 
     def step(n, carry):
-        @pl.when(n < NQ)
+        @pl.when(n < NS)
         def _():
             for d in range(4):
                 ac(n, d).wait_recv()
@@ -258,11 +275,11 @@
             for copy in own(n, buf):
                 copy.start()
 
-            @pl.when(n + 1 < NQ)
+            @pl.when(n + 1 < NS)
             def _():
                 forward(n + 1)
 
-        @pl.when((n >= 1) & (n <= NQ))
+        @pl.when((n >= 1) & (n <= NS))
         def _():
             for d in range(1, 4):
                 for copy in p1(n - 1, 0, d):
@@ -273,32 +290,69 @@
                 for copy in p2(n - 1, d):
                     copy.start()
 
+            @pl.when(n - 1 < NF)
+            def _():
+                for copy in swap(n - 1, 0):
+                    copy.start()
+
         @pl.when(n >= 2)
         def _():
             m = n - 2
-            loads = [
-                pltpu.make_async_copy(ma.at[m, z], xv.at[z, :, :, 0:HW], lsem.at[0]),
-                pltpu.make_async_copy(mb.at[m, x], xv.at[:, x, :, HW:CW], lsem.at[1]),
-            ]
-            for load in loads:
-                load.start()
-            for d in range(1, 4):
-                for copy in p2(m, d):
-                    copy.wait_recv()
-                zs, xs = plus(z, 4 - d), plus(x, 4 - d)
-                more = [
-                    pltpu.make_async_copy(xa.at[m, zs], xv.at[zs, :, :, 0:HW], lsem.at[2 * d]),
-                    pltpu.make_async_copy(xb.at[m, xs], xv.at[:, xs, :, HW:CW], lsem.at[2 * d + 1]),
+            swapped = (m == NS - 1) | (m == NS + 1)
+            first = pltpu.make_async_copy
+
+            @pl.when(jnp.logical_not(swapped))
+            def _():
+                i = jnp.minimum(m, NS - 1)
+                loads = [
+                    first(ma.at[i, z], xv.at[z, :, :, 0:HW], lsem.at[0]),
+                    first(mb.at[i, x], xv.at[:, x, :, HW:CW], lsem.at[1]),
                 ]
-                for load in more:
+                for load in loads:
                     load.start()
-                loads += more
-            for load in loads:
-                load.wait()
+                for d in range(1, 4):
+                    for copy in p2(i, d):
+                        copy.wait_recv()
+
+                    @pl.when(i < NF)
+                    def _():
+                        for copy in swap(i, d):
+                            copy.start()
+
+                    zs, xs = plus(z, 4 - d), plus(x, 4 - d)
+                    more = [
+                        first(xa.at[i, zs], xv.at[zs, :, :, 0:HW], lsem.at[2 * d]),
+                        first(xb.at[i, xs], xv.at[:, xs, :, HW:CW], lsem.at[2 * d + 1]),
+                    ]
+                    for load in more:
+                        load.start()
+                    loads += more
+                for load in loads:
+                    load.wait()
+
+            @pl.when(swapped)
+            def _():
+                i = (m - NS + 1) // 2
+                for d in range(4):
+                    for copy in swap(i, d):
+                        copy.wait_recv()
+                loads = []
+                for d in range(4):
+                    loads += [
+                        first(pa.at[i, d], xv.at[d, :, :, 0:HW], lsem.at[2 * d]),
+                        first(pb.at[i, d], xv.at[:, d, :, HW:CW], lsem.at[2 * d + 1]),
+                    ]
+                for load in loads:
+                    load.start()
+                for load in loads:
+                    load.wait()
+
+            i = jnp.where(swapped, (m - NS + 1) // 2, jnp.minimum(m, NS - 1))
+            chunk = fetched(i, jnp.where(swapped, 1 - parity, parity))
             for i in range(4):
                 rows = xv[i].reshape(4 * SLAB, CW)
-                gate[i] += jnp.dot(rows, wg[m], preferred_element_type=f32)
-                up[i] += jnp.dot(rows, wu[m], preferred_element_type=f32)
+                gate[i] += jnp.dot(rows, wg[chunk], preferred_element_type=f32)
+                up[i] += jnp.dot(rows, wu[chunk], preferred_element_type=f32)
 
         return carry
 
@@ -316,8 +370,12 @@
             ac(n, d).wait_send()
         return carry
 
-    lax.fori_loop(0, NQ, finish, 0)
-    for n in range(NQ - NB, NQ):
+    lax.fori_loop(0, NS, finish, 0)
+    for n in range(NF):
+        for d in range(4):
+            for copy in swap(n, d):
+                copy.wait_send()
+    for n in range(NS - NB, NS):
         for d in range(1, 4):
             for copy in p1(n, n % NB, d):
                 copy.wait_send()
@@ -326,8 +384,8 @@
 def return_kernel(
     inner, meta, resid, wd_hbm,
     out, ra, rb, ya, yb,
-    places, slots, weights, sr, wd, rv, total, half, core_in, mix, y_in,
-    p1_ss, p1_rs, p2_ss, p2_rs, rc_ss, rc_rs, ry_ss, ry_rs, loc, wsem, lsem,
+    places, slots, weights, sr, sw_out, sw_in, wd, rv, total, half, core_in, mix, y_in,
+    p1_ss, p1_rs, p2_ss, p2_rs, rc_ss, rc_rs, ry_ss, ry_rs, sw_ss, sw_rs, loc, wsem, lsem,
 ):
     x, c, z, y = coords()
     core = place(x, 1 - c, z, y)
@@ -368,10 +426,27 @@
             mix.at[lax.rem(n, 2), plus(y, d)], y_in.at[n, d - 1], ry_ss.at[n, d - 1], ry_rs.at[n, d - 1], ypeer[d - 1]
         )
 
+    parity = lax.rem(y, 2)
+    pair = place(x, c, z, y + 1 - 2 * parity)
+
+    def swap(i):
+        return remote(sw_out.at[i], sw_in.at[i], sw_ss.at[i], sw_rs.at[i], pair)
+
+    def down(i, chunk):
+        cols = pl.ds(pl.multiple_of(chunk * CW, CW), CW)
+        return jnp.dot(inner[i], wd[:, cols], preferred_element_type=f32)
+
+    def start_swap(n):
+        for i in range(4):
+            part = down(i, 2 * n + 1 - parity).astype(bf16)
+            sw_out[n, i] = part.reshape(4, SLAB, CW)
+        swap(n).start()
+
     load_wd.wait()
+    start_swap(0)
 
     def step(n, carry):
-        @pl.when(n < NQ)
+        @pl.when(n < NS)
         def _():
             buf = lax.rem(n, NB)
 
@@ -381,10 +456,20 @@
                     for copy in p1(n - NB, buf, d):
                         copy.wait_send()
 
-            down = wd[:, pl.ds(pl.multiple_of(n * CW, CW), CW)]
-            for i in range(4):
-                part = jnp.dot(inner[i], down, preferred_element_type=f32).astype(bf16)
-                sr[buf, i] = part.reshape(4, SLAB, CW)
+            @pl.when(n < NS - NF)
+            def _():
+                for i in range(4):
+                    part = down(i, 2 * NF + n)
+                    sr[buf, i] = part.astype(bf16).reshape(4, SLAB, CW)
+
+            @pl.when(n >= NS - NF)
+            def _():
+                at = n - (NS - NF)
+                swap(at).wait_recv()
+                for i in range(4):
+                    part = down(i, 2 * at + parity).reshape(4, SLAB, CW)
+                    sr[buf, i] = (part + sw_in[at, i].astype(f32)).astype(bf16)
+
             for d in range(1, 4):
                 for copy in p1(n, buf, d):
                     copy.start()
@@ -393,10 +478,12 @@
 
         @pl.when(n == 0)
         def _():
+            for i in range(1, NF):
+                start_swap(i)
             find_slots(meta, slots, weights, c, y)
             fill_places(slots, weights, places)
 
-        @pl.when((n >= 1) & (n <= NQ))
+        @pl.when((n >= 1) & (n <= NS))
         def _():
             for d in range(1, 4):
                 for copy in p1(n - 1, 0, d):
@@ -407,7 +494,7 @@
                 for copy in p2(n - 1, d):
                     copy.start()
 
-        @pl.when((n >= 2) & (n <= NQ + 1))
+        @pl.when((n >= 2) & (n <= NS + 1))
         def _():
             m = n - 2
             loads = [
@@ -444,7 +531,7 @@
             half[lax.rem(m, 2)] = total[lax.rem(m, 2)].astype(bf16)
             rc(m).start()
 
-        @pl.when((n >= 3) & (n <= NQ + 2))
+        @pl.when((n >= 3) & (n <= NS + 2))
         def _():
             m = n - 3
             rc(m).wait_recv()
@@ -461,16 +548,28 @@
         @pl.when(n >= 4)
         def _():
             m = n - 4
-            value = mix[lax.rem(m, 2), y].astype(f32)
             for d in range(1, 4):
                 ry(m, d).wait_recv()
-                value += y_in[m, d - 1].astype(f32)
-            cols = pl.ds(pl.multiple_of(m * CW, CW), CW)
-            out[:, cols] = (resid[:, cols].astype(f32) + value).astype(bf16)
+            own_part = mix[lax.rem(m, 2), y].astype(f32)
+            one, two, three = [y_in[m, i].astype(f32) for i in range(3)]
+
+            def put(chunk, value):
+                cols = pl.ds(pl.multiple_of(chunk * CW, CW), CW)
+                out[:, cols] = (resid[:, cols].astype(f32) + value).astype(bf16)
+
+            @pl.when(m < NS - NF)
+            def _():
+                put(2 * NF + m, own_part + one + two + three)
+
+            @pl.when(m >= NS - NF)
+            def _():
+                at = 2 * (m - (NS - NF))
+                put(at + parity, own_part + two)
+                put(at + 1 - parity, one + three)
 
         return carry
 
-    lax.fori_loop(0, NQ + 4, step, 0)
+    lax.fori_loop(0, NS + 4, step, 0)
 
     def finish(n, carry):
         for d in range(1, 4):
@@ -478,15 +577,17 @@
                 copy.wait_send()
         return carry
 
-    lax.fori_loop(0, NQ, finish, 0)
-    for n in range(NQ - NB, NQ):
+    lax.fori_loop(0, NS, finish, 0)
+    for n in range(NS - NB, NS):
         for d in range(1, 4):
             for copy in p1(n, n % NB, d):
                 copy.wait_send()
-    for n in range(NQ - 2, NQ):
+    for n in range(NS - 2, NS):
         rc(n).wait_send()
         for d in range(1, 4):
             ry(n, d).wait_send()
+    for n in range(NF):
+        swap(n).wait_send()
 
 
 VM = pl.BlockSpec(memory_space=pltpu.VMEM)
@@ -528,14 +629,15 @@
         compiler_params=params(0),
     )(hidden_in, queries, key_rows, value_rows, doc_row, docs[:, None], meta, norm_gain[None, :])
 
-    landing = jax.ShapeDtypeStruct((NQ, 4, 4, SLAB, HW), bf16)
+    landing = jax.ShapeDtypeStruct((NS, 4, 4, SLAB, HW), bf16)
+    swapped = jax.ShapeDtypeStruct((NF, 4, 4, SLAB, HW), bf16)
     inner, *_ = pl.pallas_call(
         expert_kernel,
-        out_shape=(jax.ShapeDtypeStruct((4, 4 * SLAB, FF_HALF), bf16),) + (landing,) * 4,
+        out_shape=(jax.ShapeDtypeStruct((4, 4 * SLAB, FF_HALF), bf16),) + (landing,) * 4 + (swapped,) * 2,
         in_specs=[VM, VM, ANY, ANY],
-        out_specs=(VM,) + (ANY,) * 4,
+        out_specs=(VM,) + (ANY,) * 6,
         scratch_shapes=[
-            pltpu.VMEM((NQ, 8, TOK, CW), bf16),
+            pltpu.VMEM((NS, 8, TOK, CW), bf16),
             pltpu.VMEM((16, SLAB, 8 * TOK), bf16),
             pltpu.VMEM((16, 8, TOK), f32),
             pltpu.VMEM((NB, 4, 4, SLAB, HW), bf16),
@@ -545,9 +647,9 @@
             pltpu.VMEM((NQ, CW, FF_HALF), bf16),
             pltpu.VMEM((NQ, CW, FF_HALF), bf16),
             pltpu.VMEM((4, 4, SLAB, CW), bf16),
-            dma(NQ, 3), dma(NQ, 3), dma(NQ, 4), dma(NQ, 4),
-            dma(NQ, 2, 3), dma(NQ, 2, 3), dma(NQ, 2, 3), dma(NQ, 2, 3),
-            dma(NQ, 2), dma(2), dma(8),
+            dma(NS, 3), dma(NS, 3), dma(NS, 4), dma(NS, 4),
+            dma(NS, 2, 3), dma(NS, 2, 3), dma(NS, 2, 3), dma(NS, 2, 3),
+            dma(NF, 2, 4), dma(NF, 2, 4), dma(NS, 2), dma(2), dma(8),
         ],
         compiler_params=params(1),
     )(nrm, meta_all, w_gate.reshape(NQ, CW, FF_HALF), w_up.reshape(NQ, CW, FF_HALF))
@@ -562,16 +664,18 @@
             pltpu.VMEM((16, 8, TOK), f32),
             pltpu.VMEM((16, 8, TOK), f32),
             pltpu.VMEM((NB, 4, 4, SLAB, CW), bf16),
+            pltpu.VMEM((NF, 4, 4, SLAB, CW), bf16),
+            pltpu.VMEM((NF, 4, 4, SLAB, CW), bf16),
             pltpu.VMEM((FF_HALF, D), bf16),
             pltpu.VMEM((4, 4, SLAB, CW), bf16),
             pltpu.VMEM((2, 2, 4, TOK, CW), f32),
             pltpu.VMEM((2, 2, 4, TOK, CW), bf16),
-            pltpu.VMEM((NQ, 4, TOK, CW), bf16),
+            pltpu.VMEM((NS, 4, TOK, CW), bf16),
             pltpu.VMEM((2, 4, TOK, CW), bf16),
-            pltpu.VMEM((NQ, 3, TOK, CW), bf16),
-            dma(NQ, 2, 3), dma(NQ, 2, 3), dma(NQ, 2, 3), dma(NQ, 2, 3),
-            dma(NQ), dma(NQ), dma(NQ, 3), dma(NQ, 3),
-            dma(NQ, 2), pltpu.SemaphoreType.DMA, dma(8),
+            pltpu.VMEM((NS, 3, TOK, CW), bf16),
+            dma(NS, 2, 3), dma(NS, 2, 3), dma(NS, 2, 3), dma(NS, 2, 3),
+            dma(NS), dma(NS), dma(NS, 3), dma(NS, 3),
+            dma(NF), dma(NF), dma(NS, 2), pltpu.SemaphoreType.DMA, dma(8),
         ],
         compiler_params=params(2),
     )(inner, meta_all, resid, w_down.reshape(FF_HALF, D))

time: 463 us -> 381 us (0.82)
  Pallas kernels: 455 us -> 373 us
    pallas_call x1, Pallas kernels: 212 us -> 167 us  [on_device(): pl.pallas_call(expert_kernel, out_shape=(jax.ShapeDtypeStruct((4, 4 * SLA...]
    pallas_call x1, Pallas kernels: 210 us -> 173 us  [on_device(): pl.pallas_call(return_kernel, out_shape=(jax.ShapeDtypeStruct((TOK, D), b...]
where the time goes in v2:
time: 381 us; the launch traced here: 380 us
  Pallas kernels  373 us (98%)
  local copies, waits for them, and re-layouts  4.82 us (1%)
    pallas_call x1, Pallas kernels, on_device(): pl.pallas_call(return_kernel, out_shape=(jax.ShapeDtypeStruct((TOK, D), b...  173 us
    pallas_call x1, Pallas kernels, on_device(): pl.pallas_call(expert_kernel, out_shape=(jax.ShapeDtypeStruct((4, 4 * SLA...  167 us
    pallas_call x1, Pallas kernels, on_device(): pl.pallas_call(attend_kernel, out_shape=(jax.ShapeDtypeStruct((TOK, D), b...  32.9 us

profile of v2, /device:TPU:0, one launch (start us, length us, event | category | flops | bytes accessed | tf_op | source)
XLA Modules:
  0.0 380.2 jit_solution(5297093999796025507)
XLA Ops:
  0.0 0.7 convert_bitcast_fusion.1
  0.7 0.6 broadcast_in_dim.12.doc_row
  1.3 0.7 convert_bitcast_fusion
  1.9 1.3 pad_maximum_fusion.meta
  3.2 1.3 broadcast_in_dim.14.gain
  4.6 0.7 copy.12.doc_col
  5.3 32.9 %shard_map.109 = (bf16[128,3584]{1,0:T(8,128)(2,1)}, bf16[7,128,512]{2,1,0:T(8,128)(2,1)}, f32[8,16,128]{2,1,0:T(8,128)}) custom-call(bf16[128,3584]{1,0:T(8,128)(2,1)} %hid.1, bf16[128,3584]{1,0:T(8,128)(2,1)} %q.1, bf16[128,512]{1,0:T(8,128)(2,1)} %k.1, bf16[128,512]{1,0:T(8,128)(2,1)} %v.1, f32[8,128]{1,0:T(8,128)} %broadcast_in_dim.12.doc_row, ...), custom_call_target="tpu_custom_call" | custom-call | tf_op jit(solution)/shard_map/pallas_call | solution.py:614
  38.2 166.9 %shard_map.110 = (bf16[4,576,640]{2,1,0:T(8,128)(2,1)}, bf16[5,4,4,144,256]{4,3,2,1,0:T(8,128)(2,1)}, bf16[5,4,4,144,256]{4,3,2,1,0:T(8,128)(2,1)}, bf16[5,4,4,1...) custom-call(bf16[7,128,512]{2,1,0:T(8,128)(2,1)} %get-tuple-element., ...), custom_call_target="tpu_custom_call" | custom-call | tf_op jit(solution)/shard_map/pallas_call | solution.py:634
  205.0 173.0 %shard_map.111 = (bf16[128,3584]{1,0:T(8,128)(2,1)}, bf16[5,4,4,144,256]{4,3,2,1,0:T(8,128)(2,1)}, bf16[5,4,4,144,256]{4,3,2,1,0:T(8,128)(2,1)}, bf16[5,4,4,144,...) custom-call(bf16[4,576,640]{2,1,0:T(8,128)(2,1)} %get-tuple-element.12.inner, f32[8,16,128]{2,1,0:T(8,128)} %get-tuple-element.11.meta, ...), custom_call_target="tpu_custom_call" | custom-call | tf_op jit(solution)/shard_map/pallas_call | solution.py:657
  378.1 2.2 copy.14

commit v3 on v2

v3 whole, which is shorter than its diff:
```python
import jax
import jax.numpy as jnp
from jax import lax
from jax.experimental import pallas as pl
from jax.experimental.pallas import tpu as pltpu
from jax.sharding import PartitionSpec as P

D = 3584
KV_HEADS = 4
HEAD_DIM = 128
TOPK = 8
WINDOW = 4
GROUP = 7
TOK = 128
CAP = 17
FF_HALF = 640
NQ = 7
CW = D // NQ
HW = CW // 2
SLAB = 144
OUT_AHEAD = 1
BACK_AHEAD = 2
NF = 2
NS = NQ - NF

MESH = pl.DeviceIdType.MESH
masked_score = -1e30
bf16 = jnp.bfloat16
f32 = jnp.float32


def coords():
    ctx, ex = lax.axis_index("ctx"), lax.axis_index("exp")
    return ctx // 2, ctx % 2, ex // 4, ex % 4


def place(x, c, z, y):
    return (x * 2 + c, z * 4 + y)


def greet(partners):
    barrier = pltpu.get_barrier_semaphore()
    for partner in partners:
        pl.semaphore_signal(barrier, inc=1, device_id=partner, device_id_type=MESH)
    pl.semaphore_wait(barrier, len(partners))


def remote(src, dst, send_sem, recv_sem, device):
    return pltpu.make_async_remote_copy(
        src_ref=src,
        dst_ref=dst,
        send_sem=send_sem,
        recv_sem=recv_sem,
        device_id=device,
        device_id_type=MESH,
    )


def fetched(n, parity):
    return jnp.where(n < NF, 2 * n + parity, n + NF)


def plus(value, steps):
    return lax.rem(value + steps, 4)


def attend(
    x, c, z, y, rank, hid, q, k, v, doc, ids, route, gain, resid_out, nrm, meta_all,
    kw, vw, docw, meta, halo_ss, halo_rs, doc_ss, doc_rs, meta_ss, meta_rs, by_rank, peers,
):
    mine = c * 4 + y
    row = jnp.broadcast_to(doc[...].astype(f32), (TOK, TOK))
    docw[WINDOW - 1] = row[0:8]
    meta[0:TOPK] = ids[...].astype(f32)
    meta[TOPK:] = route[...]

    def send_doc(d):
        return remote(
            docw.at[WINDOW - 1], docw.at[WINDOW - 1 - d], doc_ss.at[d - 1], doc_rs.at[d - 1], by_rank(d)
        )

    def send_head(g, d):
        cols = pl.ds(g * HEAD_DIM, HEAD_DIM)
        return [
            remote(
                src.at[:, cols], dst.at[g, WINDOW - 1 - d], halo_ss.at[g, d - 1, i], halo_rs.at[g, d - 1, i], by_rank(d)
            )
            for i, (src, dst) in enumerate(((k, kw), (v, vw)))
        ]

    def send_meta(i):
        return remote(meta, meta_all.at[mine], meta_ss.at[i], meta_rs.at[i], peers[i])

    for d in range(1, WINDOW):
        send_doc(d).start()
    for g in range(KV_HEADS):
        for d in range(1, WINDOW):
            for copy in send_head(g, d):
                copy.start()
    for i in range(7):
        send_meta(i).start()
    meta_all[mine] = meta[...]
    for g in range(KV_HEADS):
        cols = slice(g * HEAD_DIM, (g + 1) * HEAD_DIM)
        kw[g, WINDOW - 1] = k[:, cols]
        vw[g, WINDOW - 1] = v[:, cols]
    for d in range(1, WINDOW):
        send_doc(d).wait_recv()

    key_doc = jnp.concatenate([docw[i][0:1, :] for i in range(WINDOW)], 1)
    span = WINDOW * TOK
    column = row.T
    query_doc = jnp.concatenate([column] * WINDOW, 1)
    key_pos = lax.broadcasted_iota(jnp.int32, (TOK, span), 1) + (rank - (WINDOW - 1)) * TOK
    query_pos = lax.broadcasted_iota(jnp.int32, (TOK, span), 0) + rank * TOK
    visible = (query_doc == key_doc) & (key_pos <= query_pos) & (key_pos >= 0)
    square = jnp.zeros((TOK, 1), f32)
    for g in range(KV_HEADS):
        for d in range(1, WINDOW):
            for copy in send_head(g, d):
                copy.wait_recv()
        keys = kw[g].reshape(span, HEAD_DIM)
        values = vw[g].reshape(span, HEAD_DIM)
        for h in range(GROUP):
            at = (g * GROUP + h) * HEAD_DIM
            here = slice(at, at + HEAD_DIM)
            scores = lax.dot_general(
                q[:, here], keys, (((1,), (1,)), ((), ())), preferred_element_type=f32
            ) * (HEAD_DIM ** -0.5)
            scores = jnp.where(visible, scores, masked_score)
            exps = jnp.exp(scores - jnp.max(scores, 1, keepdims=True))
            probs = (exps / jnp.sum(exps, 1, keepdims=True)).astype(bf16)
            context = jnp.dot(probs, values, preferred_element_type=f32).astype(bf16)
            resid = (hid[:, here].astype(f32) + context.astype(f32)).astype(bf16)
            resid_out[:, here] = resid
            resid_f = resid.astype(f32)
            square += jnp.sum(resid_f * resid_f, 1, keepdims=True)
    inverse = lax.rsqrt(square * (1.0 / D) + 1e-06)
    for n in range(NQ):
        cols = slice(n * CW, (n + 1) * CW)
        nrm[n] = (resid_out[:, cols].astype(f32) * inverse * gain[:, cols]).astype(bf16)
    for i in range(7):
        send_meta(i).wait_recv()

    def finish():
        for d in range(1, WINDOW):
            send_doc(d).wait_send()
        for g in range(KV_HEADS):
            for d in range(1, WINDOW):
                for copy in send_head(g, d):
                    copy.wait_send()
        for i in range(7):
            send_meta(i).wait_send()

    return finish


def find_slots(meta, slots, weights, c, y):
    s = lax.broadcasted_iota(jnp.int32, (16, TOPK, TOK), 0)
    expert = (((s >> 2) * 2 + c) * 8 + (s & 3) * 2 + (y >> 1)).astype(f32)
    earlier = lax.broadcasted_iota(jnp.int32, (TOK, TOK), 0) < lax.broadcasted_iota(
        jnp.int32, (TOK, TOK), 1
    )
    earlier = jnp.where(earlier, 1.0, 0.0).astype(bf16)
    for b in range(8):
        ids = meta[b][0:TOPK, :]
        hit = ids[None] == expert
        member = jnp.sum(jnp.where(hit, 1.0, 0.0), 1)
        before = jnp.dot(member.astype(bf16), earlier, preferred_element_type=f32)
        slots[:, b, :] = jnp.where(member > 0.5, before + float(CAP * b), -1.0)
        if weights is not None:
            weights[:, b, :] = jnp.sum(jnp.where(hit, meta[b][TOPK:, :][None], 0.0), 1)


def fill_places(slots, weights, out):
    def one(s, carry):
        rows = lax.broadcasted_iota(jnp.int32, (SLAB, TOK), 0).astype(f32)
        slot = slots[s]
        weight = None if weights is None else weights[s]
        for b in range(8):
            value = 1.0 if weight is None else weight[b : b + 1, :]
            out[s, :, b * TOK : (b + 1) * TOK] = jnp.where(
                rows == slot[b : b + 1, :], value, 0.0
            ).astype(bf16)
        return carry

    lax.fori_loop(0, 16, one, 0)


def expert_kernel(
    hid, q, k, v, doc, ids, route, gain, wg_hbm, wu_hbm,
    resid_out, meta_all, inner_out, ma, mb, xa, xb, pa, pb,
    kw, vw, docw, meta, halo_ss, halo_rs, doc_ss, doc_rs, meta_ss, meta_rs, nrm, tok, places, slots, sa, sb, gate, up, wg, wu, xv,
    ay_ss, ay_rs, ac_ss, ac_rs, p1_ss, p1_rs, p2_ss, p2_rs, sw_ss, sw_rs, loc, wsem, lsem,
):
    x, c, z, y = coords()
    core = place(x, 1 - c, z, y)
    ypeer = [place(x, c, z, plus(y, d)) for d in range(1, 4)]
    xpeer = [place(plus(x, d), c, z, y) for d in range(1, 4)]
    zpeer = [place(x, c, plus(z, d), y) for d in range(1, 4)]
    rank = lax.axis_index("ctx") * 16 + lax.axis_index("exp")

    def by_rank(steps):
        other = lax.rem(rank + steps + 128, 128)
        return (other // 16, lax.rem(other, 16))

    peers = [core] + ypeer + [place(x, 1 - c, z, plus(y, d)) for d in range(1, 4)]
    weights = [
        pltpu.make_async_copy(wg_hbm, wg, wsem.at[0]),
        pltpu.make_async_copy(wu_hbm, wu, wsem.at[1]),
    ]
    for copy in weights:
        copy.start()

    greet([by_rank(d) for d in (1, 2, 3, -1, -2, -3)] + peers + xpeer + zpeer)
    finish_attend = attend(
        x, c, z, y, rank, hid, q, k, v, doc, ids, route, gain, resid_out, nrm, meta_all,
        kw, vw, docw, meta, halo_ss, halo_rs, doc_ss, doc_rs, meta_ss, meta_rs, by_rank, peers,
    )
    mine = c * 4 + y
    parity = lax.rem(y, 2)
    pair = place(x, c, z, y + 1 - 2 * parity)

    def ay(n, d):
        src = nrm.at[fetched(n, lax.rem(y + d, 2))]
        return remote(src, tok.at[n, mine], ay_ss.at[n, d - 1], ay_rs.at[n, d - 1], ypeer[d - 1])

    def ac(n, d):
        if d == 0:
            src = nrm.at[fetched(n, parity)]
            at = mine
        else:
            at = c * 4 + plus(y, 4 - d)
            src = tok.at[n, at]
        return remote(src, tok.at[n, at], ac_ss.at[n, d], ac_rs.at[n, d], core)

    def p1(n, d):
        xp, zp = plus(x, d), plus(z, d)
        return (
            remote(sa.at[n, xp], ma.at[n, :, x], p1_ss.at[n, 0, d - 1], p1_rs.at[n, 0, d - 1], xpeer[d - 1]),
            remote(sb.at[n, zp], mb.at[n, :, z], p1_ss.at[n, 1, d - 1], p1_rs.at[n, 1, d - 1], zpeer[d - 1]),
        )

    def own(n):
        return (
            pltpu.make_async_copy(sa.at[n, x], ma.at[n, :, x], loc.at[n, 0]),
            pltpu.make_async_copy(sb.at[n, z], mb.at[n, :, z], loc.at[n, 1]),
        )

    def p2(n, d):
        xp, zp = plus(x, d), plus(z, d)
        return (
            remote(ma.at[n, zp], xa.at[n, z], p2_ss.at[n, 0, d - 1], p2_rs.at[n, 0, d - 1], zpeer[d - 1]),
            remote(mb.at[n, xp], xb.at[n, x], p2_ss.at[n, 1, d - 1], p2_rs.at[n, 1, d - 1], xpeer[d - 1]),
        )

    def swap(n, d):
        zs, xs = plus(z, 4 - d), plus(x, 4 - d)
        a, b = (ma.at[n, z], mb.at[n, x]) if d == 0 else (xa.at[n, zs], xb.at[n, xs])
        return (
            remote(a, pa.at[n, zs], sw_ss.at[n, 0, d], sw_rs.at[n, 0, d], pair),
            remote(b, pb.at[n, xs], sw_ss.at[n, 1, d], sw_rs.at[n, 1, d], pair),
        )

    def start_gather(n):
        for d in range(1, 4):
            ay(n, d).start()
        ac(n, 0).start()
        tok[n, mine] = nrm[fetched(n, parity)]

    start_gather(0)

    def forward(n):
        for d in range(1, 4):
            ay(n, d).wait_recv()
            ac(n, d).start()

    find_slots(meta_all, slots, None, c, y)
    fill_places(slots, None, places)
    forward(0)
    start_gather(1)
    gate[...] = jnp.zeros_like(gate)
    up[...] = jnp.zeros_like(up)
    for copy in weights:
        copy.wait()

    def step(n, carry):
        @pl.when(n < NS)
        def _():
            for d in range(4):
                ac(n, d).wait_recv()
            chunk = tok[n].reshape(8 * TOK, CW)
            for xp in range(4):
                rows = places[xp * 4 : xp * 4 + 4].reshape(4 * SLAB, 8 * TOK)
                packed = jnp.dot(rows, chunk, preferred_element_type=f32).astype(bf16)
                packed = packed.reshape(4, SLAB, CW)
                sa[n, xp] = packed[:, :, :HW]
                sb[n, :, xp] = packed[:, :, HW:]
            for d in range(1, 4):
                for copy in p1(n, d):
                    copy.start()
            for copy in own(n):
                copy.start()

            @pl.when(n + 1 < NS)
            def _():
                forward(n + 1)

            @pl.when(n + 2 < NS)
            def _():
                start_gather(n + 2)

        @pl.when((n >= OUT_AHEAD) & (n < NS + OUT_AHEAD))
        def _():
            i = n - OUT_AHEAD
            for d in range(1, 4):
                for copy in p1(i, d):
                    copy.wait_recv()
            for copy in own(i):
                copy.wait()
            for d in range(1, 4):
                for copy in p2(i, d):
                    copy.start()

            @pl.when(i < NF)
            def _():
                for copy in swap(i, 0):
                    copy.start()

        @pl.when((n > OUT_AHEAD) & (n <= OUT_AHEAD + NF))
        def _():
            i = n - OUT_AHEAD - 1
            for d in range(1, 4):
                for copy in p2(i, d):
                    copy.wait_recv()
                for copy in swap(i, d):
                    copy.start()

        @pl.when(n >= OUT_AHEAD + 2)
        def _():
            m = n - OUT_AHEAD - 2
            swapped = (m == NS - 1) | (m == NS + 1)
            first = pltpu.make_async_copy

            @pl.when(jnp.logical_not(swapped))
            def _():
                i = jnp.minimum(m, NS - 1)
                loads = [
                    first(ma.at[i, z], xv.at[z, :, :, 0:HW], lsem.at[0]),
                    first(mb.at[i, x], xv.at[:, x, :, HW:CW], lsem.at[1]),
                ]
                for load in loads:
                    load.start()
                for d in range(1, 4):
                    @pl.when(i >= NF)
                    def _():
                        for copy in p2(i, d):
                            copy.wait_recv()

                    zs, xs = plus(z, 4 - d), plus(x, 4 - d)
                    more = [
                        first(xa.at[i, zs], xv.at[zs, :, :, 0:HW], lsem.at[2 * d]),
                        first(xb.at[i, xs], xv.at[:, xs, :, HW:CW], lsem.at[2 * d + 1]),
                    ]
                    for load in more:
                        load.start()
                    loads += more
                for load in loads:
                    load.wait()

            @pl.when(swapped)
            def _():
                i = (m - NS + 1) // 2
                for d in range(4):
                    for copy in swap(i, d):
                        copy.wait_recv()
                loads = []
                for d in range(4):
                    loads += [
                        first(pa.at[i, d], xv.at[d, :, :, 0:HW], lsem.at[2 * d]),
                        first(pb.at[i, d], xv.at[:, d, :, HW:CW], lsem.at[2 * d + 1]),
                    ]
                for load in loads:
                    load.start()
                for load in loads:
                    load.wait()

            i = jnp.where(swapped, (m - NS + 1) // 2, jnp.minimum(m, NS - 1))
            chunk = fetched(i, jnp.where(swapped, 1 - parity, parity))
            for i in range(4):
                rows = xv[i].reshape(4 * SLAB, CW)
                gate[i] += jnp.dot(rows, wg[chunk], preferred_element_type=f32)
                up[i] += jnp.dot(rows, wu[chunk], preferred_element_type=f32)

        return carry

    lax.fori_loop(0, NQ + OUT_AHEAD + 2, step, 0)
    for i in range(4):
        value = gate[i]
        inner_out[i] = (value / (1.0 + jnp.exp(-value)) * up[i]).astype(bf16)

    def finish(n, carry):
        for d in range(1, 4):
            ay(n, d).wait_send()
            for copy in p1(n, d) + p2(n, d):
                copy.wait_send()
        for d in range(4):
            ac(n, d).wait_send()
        return carry

    lax.fori_loop(0, NS, finish, 0)
    for n in range(NF):
        for d in range(4):
            for copy in swap(n, d):
                copy.wait_send()
    finish_attend()


def return_kernel(
    inner, meta, resid, wd_hbm,
    out, ra, rb, ya, yb,
    places, slots, weights, sr, sw_out, sw_in, wd, rv, total, half, core_in, mix, y_in,
    p1_ss, p1_rs, p2_ss, p2_rs, rc_ss, rc_rs, ry_ss, ry_rs, sw_ss, sw_rs, loc, wsem, lsem,
):
    x, c, z, y = coords()
    core = place(x, 1 - c, z, y)
    ypeer = [place(x, c, z, plus(y, d)) for d in range(1, 4)]
    xpeer = [place(plus(x, d), c, z, y) for d in range(1, 4)]
    zpeer = [place(x, c, plus(z, d), y) for d in range(1, 4)]
    load_wd = pltpu.make_async_copy(wd_hbm, wd, wsem)
    load_wd.start()
    greet([core] + ypeer + xpeer + zpeer)

    def p1_z(n, d):
        zp = plus(z, d)
        return remote(
            sr.at[n, zp, :, :, 0:HW], ra.at[n, :, z], p1_ss.at[n, 0, d - 1], p1_rs.at[n, 0, d - 1], zpeer[d - 1]
        )

    def p1(n, d):
        xp = plus(x, d)
        return (
            p1_z(n, d),
            remote(sr.at[n, :, xp, :, HW:CW], rb.at[n, :, x], p1_ss.at[n, 1, d - 1], p1_rs.at[n, 1, d - 1], xpeer[d - 1]),
        )

    def p1_part(n, i, d):
        xp = plus(x, d)
        return remote(
            sr.at[n, i, xp, :, HW:CW], rb.at[n, i, x], p1_ss.at[n, 1, d - 1], p1_rs.at[n, 1, d - 1], xpeer[d - 1]
        )

    def own(n):
        return (
            pltpu.make_async_copy(sr.at[n, z, :, :, 0:HW], ra.at[n, :, z], loc.at[n, 0]),
            pltpu.make_async_copy(sr.at[n, :, x, :, HW:CW], rb.at[n, :, x], loc.at[n, 1]),
        )

    def p2(n, d):
        xp, zp = plus(x, d), plus(z, d)
        return (
            remote(ra.at[n, xp], ya.at[n, x], p2_ss.at[n, 0, d - 1], p2_rs.at[n, 0, d - 1], xpeer[d - 1]),
            remote(rb.at[n, zp], yb.at[n, z], p2_ss.at[n, 1, d - 1], p2_rs.at[n, 1, d - 1], zpeer[d - 1]),
        )

    def rc(n):
        return remote(
            half.at[lax.rem(n, 2), 1 - c], core_in.at[n], rc_ss.at[n], rc_rs.at[n], core
        )

    def ry(n, d):
        return remote(
            mix.at[n, plus(y, d)], y_in.at[n, d - 1], ry_ss.at[n, d - 1], ry_rs.at[n, d - 1], ypeer[d - 1]
        )

    parity = lax.rem(y, 2)
    pair = place(x, c, z, y + 1 - 2 * parity)
    other = place(x, c, z, plus(y, 3 + 2 * parity))

    def ry_by(n, to, device):
        d = lax.rem(to - y + 4, 4)
        return remote(
            mix.at[n, to], y_in.at[n, d - 1], ry_ss.at[n, d - 1], ry_rs.at[n, d - 1], device
        )

    def ry_pair(n):
        return ry_by(n, y + 1 - 2 * parity, pair)

    def ry_far(n):
        return ry_by(n, plus(y, 3 + 2 * parity), other)

    def swap(f, d):
        i = plus(z, d)
        return remote(sw_out.at[f, i], sw_in.at[f, i], sw_ss.at[f, d], sw_rs.at[f, d], pair)

    def down(i, chunk):
        cols = pl.ds(pl.multiple_of(chunk * CW, CW), CW)
        return jnp.dot(inner[i], wd[:, cols], preferred_element_type=f32)

    order = (1, 2, 3, 0)

    def start_swap(f):
        for d in order:
            i = plus(z, d)
            part = down(i, 2 * f + 1 - parity).astype(bf16)
            sw_out[f, i] = part.reshape(4, SLAB, CW)
            swap(f, d).start()

    load_wd.wait()
    start_swap(0)

    def step(n, carry):
        @pl.when(n < NS - NF)
        def _():
            for i in range(4):
                part = down(i, 2 * NF + n)
                sr[n, i] = part.astype(bf16).reshape(4, SLAB, CW)
            for d in range(1, 4):
                for copy in p1(n, d):
                    copy.start()
            for copy in own(n):
                copy.start()

        @pl.when(n == 0)
        def _():
            for f in range(1, NF):
                start_swap(f)
            find_slots(meta, slots, weights, c, y)
            fill_places(slots, weights, places)

        @pl.when((n >= BACK_AHEAD) & (n < NS + BACK_AHEAD))
        def _():
            i = n - BACK_AHEAD
            for d in range(1, 4):
                for copy in p1(i, d):
                    copy.wait_recv()
            for copy in own(i):
                copy.wait()
            for d in range(1, 4):
                for copy in p2(i, d):
                    copy.start()

        @pl.when((n >= 4) & (n < NS + 4))
        def _():
            m = n - 4
            rc(m).wait_recv()
            mix[m] = (total[lax.rem(m, 2), c] + core_in[m].astype(f32)).astype(bf16)

            @pl.when(m < 2)
            def _():
                ry_far(m).start()

            @pl.when(m == 2)
            def _():
                for i in range(2):
                    ry_pair(i).start()
                    ry(i, 2).start()

            @pl.when(m >= 2)
            def _():
                for d in range(1, 4):
                    ry(m, d).start()

        @pl.when((n >= 3) & (n < NS + 3))
        def _():
            m = n - 3
            loads = [
                pltpu.make_async_copy(ra.at[m, x], rv.at[x, :, :, 0:HW], lsem.at[0]),
                pltpu.make_async_copy(rb.at[m, z], rv.at[:, z, :, HW:CW], lsem.at[1]),
            ]
            for load in loads:
                load.start()
            for d in range(1, 4):
                for copy in p2(m, d):
                    copy.wait_recv()
                zs, xs = plus(z, 4 - d), plus(x, 4 - d)
                more = [
                    pltpu.make_async_copy(ya.at[m, xs], rv.at[xs, :, :, 0:HW], lsem.at[2 * d]),
                    pltpu.make_async_copy(yb.at[m, zs], rv.at[:, zs, :, HW:CW], lsem.at[2 * d + 1]),
                ]
                for load in more:
                    load.start()
                loads += more
            for load in loads:
                load.wait()
            moe = lax.dot_general(
                places[...].reshape(16 * SLAB, 8 * TOK),
                rv[...].reshape(16 * SLAB, CW),
                (((0,), (0,)), ((), ())),
                preferred_element_type=f32,
            )
            total[lax.rem(m, 2)] = moe.reshape(2, 4, TOK, CW)

            @pl.when(m >= 2)
            def _():
                rc(m - 2).wait_send()

            half[lax.rem(m, 2)] = total[lax.rem(m, 2)].astype(bf16)
            rc(m).start()

        @pl.when((n == NS - NF) | (n == NS))
        def _():
            f = (n - (NS - NF)) // 2
            u = NS - NF + f
            for d in order:
                swap(f, d).wait_recv()
                i = plus(z, d)
                part = down(i, 2 * f + parity).reshape(4, SLAB, CW)
                sr[u, i] = (part + sw_in[f, i].astype(f32)).astype(bf16)
                if d > 0:
                    p1_z(u, d).start()
                for e in range(1, 4):
                    p1_part(u, i, e).start()
            for copy in own(u):
                copy.start()

        return carry

    lax.fori_loop(0, NS + 4, step, 0)

    def result(m, carry):
        for d in range(1, 4):
            ry(m, d).wait_recv()
        own_part = mix[m, y].astype(f32)
        one, two, three = [y_in[m, i].astype(f32) for i in range(3)]

        def put(chunk, value):
            cols = pl.ds(pl.multiple_of(chunk * CW, CW), CW)
            out[:, cols] = (resid[:, cols].astype(f32) + value).astype(bf16)

        @pl.when(m < NS - NF)
        def _():
            put(2 * NF + m, own_part + one + two + three)

        @pl.when(m >= NS - NF)
        def _():
            at = 2 * (m - (NS - NF))
            put(at + parity, own_part + two)
            put(at + 1 - parity, one + three)
        return carry

    lax.fori_loop(0, NS, result, 0)

    def finish(n, carry):
        for d in range(1, 4):
            for copy in p1(n, d) + p2(n, d):
                copy.wait_send()
            ry(n, d).wait_send()
        return carry

    lax.fori_loop(0, NS, finish, 0)
    for n in range(NS - 2, NS):
        rc(n).wait_send()
    for f in range(NF):
        for d in range(4):
            swap(f, d).wait_send()


VM = pl.BlockSpec(memory_space=pltpu.VMEM)
ANY = pl.BlockSpec(memory_space=pl.ANY)


def dma(*shape):
    return pltpu.SemaphoreType.DMA(shape)


def params(collective_id):
    return pltpu.CompilerParams(
        collective_id=collective_id, has_side_effects=True, vmem_limit_bytes=62 << 20
    )


def on_device(
    hidden_in, queries, key_rows, value_rows, document_ids, norm_gain,
    w_gate, w_up, w_down, expert_ids, route_weights,
):
    landing = jax.ShapeDtypeStruct((NS, 4, 4, SLAB, HW), bf16)
    swapped = jax.ShapeDtypeStruct((NF, 4, 4, SLAB, HW), bf16)
    resid, meta_all, inner, *_ = pl.pallas_call(
        expert_kernel,
        out_shape=(
            jax.ShapeDtypeStruct((TOK, D), bf16),
            jax.ShapeDtypeStruct((8, 2 * TOPK, TOK), f32),
            jax.ShapeDtypeStruct((4, 4 * SLAB, FF_HALF), bf16),
        ) + (landing,) * 4 + (swapped,) * 2,
        in_specs=[VM] * 8 + [ANY] * 2,
        out_specs=(VM,) * 3 + (ANY,) * 6,
        scratch_shapes=[
            pltpu.VMEM((KV_HEADS, WINDOW, TOK, HEAD_DIM), bf16),
            pltpu.VMEM((KV_HEADS, WINDOW, TOK, HEAD_DIM), bf16),
            pltpu.VMEM((WINDOW, 8, TOK), f32),
            pltpu.VMEM((2 * TOPK, TOK), f32),
            dma(KV_HEADS, 3, 2), dma(KV_HEADS, 3, 2), dma(3), dma(3), dma(7), dma(7),
            pltpu.VMEM((NQ, TOK, CW), bf16),
            pltpu.VMEM((NS, 8, TOK, CW), bf16),
            pltpu.VMEM((16, SLAB, 8 * TOK), bf16),
            pltpu.VMEM((16, 8, TOK), f32),
            pltpu.VMEM((NS, 4, 4, SLAB, HW), bf16),
            pltpu.VMEM((NS, 4, 4, SLAB, HW), bf16),
            pltpu.VMEM((4, 4 * SLAB, FF_HALF), f32),
            pltpu.VMEM((4, 4 * SLAB, FF_HALF), f32),
            pltpu.VMEM((NQ, CW, FF_HALF), bf16),
            pltpu.VMEM((NQ, CW, FF_HALF), bf16),
            pltpu.VMEM((4, 4, SLAB, CW), bf16),
            dma(NS, 3), dma(NS, 3), dma(NS, 4), dma(NS, 4),
            dma(NS, 2, 3), dma(NS, 2, 3), dma(NS, 2, 3), dma(NS, 2, 3),
            dma(NF, 2, 4), dma(NF, 2, 4), dma(NS, 2), dma(2), dma(8),
        ],
        compiler_params=params(0),
    )(
        hidden_in, queries, key_rows, value_rows, document_ids.reshape(1, TOK), expert_ids.T,
        route_weights.T, norm_gain.reshape(1, D),
        w_gate.reshape(NQ, CW, FF_HALF), w_up.reshape(NQ, CW, FF_HALF),
    )

    out, *_ = pl.pallas_call(
        return_kernel,
        out_shape=(jax.ShapeDtypeStruct((TOK, D), bf16),) + (landing,) * 4,
        in_specs=[VM, VM, VM, ANY],
        out_specs=(VM,) + (ANY,) * 4,
        scratch_shapes=[
            pltpu.VMEM((16, SLAB, 8 * TOK), bf16),
            pltpu.VMEM((16, 8, TOK), f32),
            pltpu.VMEM((16, 8, TOK), f32),
            pltpu.VMEM((NS, 4, 4, SLAB, CW), bf16),
            pltpu.VMEM((NF, 4, 4, SLAB, CW), bf16),
            pltpu.VMEM((NF, 4, 4, SLAB, CW), bf16),
            pltpu.VMEM((FF_HALF, D), bf16),
            pltpu.VMEM((4, 4, SLAB, CW), bf16),
            pltpu.VMEM((2, 2, 4, TOK, CW), f32),
            pltpu.VMEM((2, 2, 4, TOK, CW), bf16),
            pltpu.VMEM((NS, 4, TOK, CW), bf16),
            pltpu.VMEM((NS, 4, TOK, CW), bf16),
            pltpu.VMEM((NS, 3, TOK, CW), bf16),
            dma(NS, 2, 3), dma(NS, 2, 3), dma(NS, 2, 3), dma(NS, 2, 3),
            dma(NS), dma(NS), dma(NS, 3), dma(NS, 3),
            dma(NF, 4), dma(NF, 4), dma(NS, 2), pltpu.SemaphoreType.DMA, dma(8),
        ],
        compiler_params=params(1),
    )(inner, meta_all, resid, w_down.reshape(FF_HALF, D))
    return out


def solution(mesh):
    rows = P(("ctx", "exp"), None)
    whole = P(("ctx", "exp"), None, None)
    in_specs = (
        rows, rows, rows, rows, P(("ctx", "exp")), P(), whole, whole, whole, rows, rows,
    )
    return jax.shard_map(
        on_device, mesh=mesh, in_specs=in_specs, out_specs=rows, check_vma=False
    )
```

time: 381 us -> 356 us (0.934)
  Pallas kernels: 373 us -> 352 us
    pallas_call x2 -> x1, Pallas kernels: 200 us -> 188 us  [on_device(): pl.pallas_call(expert_kernel, out_shape=(jax.ShapeDtypeStruct((TOK, D), b...]
    pallas_call x1, Pallas kernels: 173 us -> 164 us  [on_device(): pl.pallas_call(return_kernel, out_shape=(jax.ShapeDtypeStruct((TOK, D), b...]
where the time goes in v3:
time: 356 us; the launch traced here: 355 us
  Pallas kernels  352 us (99%)
    pallas_call x1, Pallas kernels, on_device(): pl.pallas_call(expert_kernel, out_shape=(jax.ShapeDtypeStruct((TOK, D), b...  188 us
    pallas_call x1, Pallas kernels, on_device(): pl.pallas_call(return_kernel, out_shape=(jax.ShapeDtypeStruct((TOK, D), b...  164 us

profile of v3, /device:TPU:0, one launch (start us, length us, event | category | flops | bytes accessed | tf_op | source)
XLA Modules:
  0.0 355.0 jit_solution(4504590233166357193)
XLA Ops:
  0.0 1.3 reshape.16.gain
  1.3 187.7 %shard_map.109 = (bf16[128,3584]{1,0:T(8,128)(2,1)}, f32[8,16,128]{2,1,0:T(8,128)}, bf16[4,576,640]{2,1,0:T(8,128)(2,1)}, bf16[5,4,4,144,256]{4,3,2,1,0:T(8,128)...) custom-call(bf16[128,3584]{1,0:T(8,128)(2,1)} %hid.1, ...), custom_call_target="tpu_custom_call" | custom-call | tf_op jit(solution)/shard_map/pallas_call | solution.py:679
  189.0 163.9 %shard_map.110 = (bf16[128,3584]{1,0:T(8,128)(2,1)}, bf16[5,4,4,144,256]{4,3,2,1,0:T(8,128)(2,1)}, bf16[5,4,4,144,256]{4,3,2,1,0:T(8,128)(2,1)}, bf16[5,4,4,144,...) custom-call(bf16[4,576,640]{2,1,0:T(8,128)(2,1)} %get-tuple-element.9.inner, f32[8,16,128]{2,1,0:T(8,128)} %get-tuple-element.10.meta, ...), custom_call_target="tpu_custom_call" | custom-call | tf_op jit(solution)/shard_map/pallas_call | solution.py:716
  352.9 2.2 copy.13

commit v4 on v3

--- a/solution.py
+++ b/solution.py
@@ -66,7 +66,7 @@
 
 def attend(
     x, c, z, y, rank, hid, q, k, v, doc, ids, route, gain, resid_out, nrm, meta_all,
-    kw, vw, docw, meta, halo_ss, halo_rs, doc_ss, doc_rs, meta_ss, meta_rs, by_rank, peers,
+    kw, vw, docw, meta, halo_ss, halo_rs, doc_ss, doc_rs, meta_ss, meta_rs, by_rank, peers, fills,
 ):
     mine = c * 4 + y
     row = jnp.broadcast_to(doc[...].astype(f32), (TOK, TOK))
@@ -93,10 +93,13 @@
 
     for d in range(1, WINDOW):
         send_doc(d).start()
-    for g in range(KV_HEADS):
+    def start_head(g):
         for d in range(1, WINDOW):
             for copy in send_head(g, d):
                 copy.start()
+
+    start_head(0)
+    start_head(1)
     for i in range(7):
         send_meta(i).start()
     meta_all[mine] = meta[...]
@@ -104,6 +107,8 @@
         cols = slice(g * HEAD_DIM, (g + 1) * HEAD_DIM)
         kw[g, WINDOW - 1] = k[:, cols]
         vw[g, WINDOW - 1] = v[:, cols]
+    for copy in fills:
+        copy.wait()
     for d in range(1, WINDOW):
         send_doc(d).wait_recv()
 
@@ -119,6 +124,8 @@
         for d in range(1, WINDOW):
             for copy in send_head(g, d):
                 copy.wait_recv()
+        if g + 2 < KV_HEADS:
+            start_head(g + 2)
         keys = kw[g].reshape(span, HEAD_DIM)
         values = vw[g].reshape(span, HEAD_DIM)
         for h in range(GROUP):
@@ -137,8 +144,11 @@
             square += jnp.sum(resid_f * resid_f, 1, keepdims=True)
     inverse = lax.rsqrt(square * (1.0 / D) + 1e-06)
     for n in range(NQ):
-        cols = slice(n * CW, (n + 1) * CW)
-        nrm[n] = (resid_out[:, cols].astype(f32) * inverse * gain[:, cols]).astype(bf16)
+        for j in range(CW // HEAD_DIM):
+            at = n * CW + j * HEAD_DIM
+            value = resid_out[:, at : at + HEAD_DIM].astype(f32) * inverse
+            tile = n * (CW // HEAD_DIM) + j
+            nrm[n, :, j * HEAD_DIM : (j + 1) * HEAD_DIM] = (value * gain[tile : tile + 1, :]).astype(bf16)
     for i in range(7):
         send_meta(i).wait_recv()
 
@@ -188,9 +198,10 @@
 
 
 def expert_kernel(
-    hid, q, k, v, doc, ids, route, gain, wg_hbm, wu_hbm,
+    hid_hbm, q_hbm, k, v, doc, ids, route, gain, wg_hbm, wu_hbm,
     resid_out, meta_all, inner_out, ma, mb, xa, xb, pa, pb,
-    kw, vw, docw, meta, halo_ss, halo_rs, doc_ss, doc_rs, meta_ss, meta_rs, nrm, tok, places, slots, sa, sb, gate, up, wg, wu, xv,
+    kw, vw, docw, meta, halo_ss, halo_rs, doc_ss, doc_rs, meta_ss, meta_rs,
+    hid, q, resid, inner, isem, rsem, osem, nrm, tok, places, slots, sa, sb, gate, up, wg, wu, xv, xlast,
     ay_ss, ay_rs, ac_ss, ac_rs, p1_ss, p1_rs, p2_ss, p2_rs, sw_ss, sw_rs, loc, wsem, lsem,
 ):
     x, c, z, y = coords()
@@ -209,14 +220,20 @@
         pltpu.make_async_copy(wg_hbm, wg, wsem.at[0]),
         pltpu.make_async_copy(wu_hbm, wu, wsem.at[1]),
     ]
-    for copy in weights:
+    fills = [
+        pltpu.make_async_copy(q_hbm, q, rsem.at[0]),
+        pltpu.make_async_copy(hid_hbm, hid, rsem.at[1]),
+    ]
+    for copy in fills + weights:
         copy.start()
 
     greet([by_rank(d) for d in (1, 2, 3, -1, -2, -3)] + peers + xpeer + zpeer)
     finish_attend = attend(
-        x, c, z, y, rank, hid, q, k, v, doc, ids, route, gain, resid_out, nrm, meta_all,
-        kw, vw, docw, meta, halo_ss, halo_rs, doc_ss, doc_rs, meta_ss, meta_rs, by_rank, peers,
+        x, c, z, y, rank, hid, q, k, v, doc, ids, route, gain, resid, nrm, meta_all,
+        kw, vw, docw, meta, halo_ss, halo_rs, doc_ss, doc_rs, meta_ss, meta_rs, by_rank, peers, fills,
     )
+    save = pltpu.make_async_copy(resid, resid_out, rsem.at[2])
+    save.start()
     mine = c * 4 + y
     parity = lax.rem(y, 2)
     pair = place(x, c, z, y + 1 - 2 * parity)
@@ -234,12 +251,18 @@
             src = tok.at[n, at]
         return remote(src, tok.at[n, at], ac_ss.at[n, d], ac_rs.at[n, d], core)
 
+    def p1_x(n, d):
+        xp = plus(x, d)
+        return remote(sa.at[n, xp], ma.at[n, :, x], p1_ss.at[n, 0, d - 1], p1_rs.at[n, 0, d - 1], xpeer[d - 1])
+
+    def p1_z(n, d):
+        zp = plus(z, d)
+        return remote(
+            sb.at[n, zp], mb.at[n, :, z], p1_ss.at[n, 1, d - 1], p1_rs.at[n, 1, d - 1], zpeer[d - 1]
+        )
+
     def p1(n, d):
-        xp, zp = plus(x, d), plus(z, d)
-        return (
-            remote(sa.at[n, xp], ma.at[n, :, x], p1_ss.at[n, 0, d - 1], p1_rs.at[n, 0, d - 1], xpeer[d - 1]),
-            remote(sb.at[n, zp], mb.at[n, :, z], p1_ss.at[n, 1, d - 1], p1_rs.at[n, 1, d - 1], zpeer[d - 1]),
-        )
+        return p1_x(n, d), p1_z(n, d)
 
     def own(n):
         return (
@@ -252,6 +275,20 @@
         return (
             remote(ma.at[n, zp], xa.at[n, z], p2_ss.at[n, 0, d - 1], p2_rs.at[n, 0, d - 1], zpeer[d - 1]),
             remote(mb.at[n, xp], xb.at[n, x], p2_ss.at[n, 1, d - 1], p2_rs.at[n, 1, d - 1], xpeer[d - 1]),
+        )
+
+    def p2_last(d):
+        n, xp, zp = NS - 1, plus(x, d), plus(z, d)
+        return (
+            remote(ma.at[n, zp], xlast.at[z, :, :, 0:HW], p2_ss.at[n, 0, d - 1], p2_rs.at[n, 0, d - 1], zpeer[d - 1]),
+            remote(mb.at[n, xp], xlast.at[:, x, :, HW:CW], p2_ss.at[n, 1, d - 1], p2_rs.at[n, 1, d - 1], xpeer[d - 1]),
+        )
+
+    def own_last():
+        n = NS - 1
+        return (
+            pltpu.make_async_copy(ma.at[n, z], xlast.at[z, :, :, 0:HW], osem.at[0]),
+            pltpu.make_async_copy(mb.at[n, x], xlast.at[:, x, :, HW:CW], osem.at[1]),
         )
 
     def swap(n, d):
@@ -269,6 +306,32 @@
         tok[n, mine] = nrm[fetched(n, parity)]
 
     start_gather(0)
+
+    local = pltpu.make_async_copy
+
+    def fetch(i, arriving):
+        def arrive(d):
+            for copy in p2(i, d):
+                copy.wait_recv()
+
+        loads = [
+            local(ma.at[i, z], xv.at[z, :, :, 0:HW], lsem.at[0]),
+            local(mb.at[i, x], xv.at[:, x, :, HW:CW], lsem.at[1]),
+        ]
+        for load in loads:
+            load.start()
+        for d in range(1, 4):
+            pl.when(arriving)(lambda: arrive(d))
+            zs, xs = plus(z, 4 - d), plus(x, 4 - d)
+            more = [
+                local(xa.at[i, zs], xv.at[zs, :, :, 0:HW], lsem.at[2 * d]),
+                local(xb.at[i, xs], xv.at[:, xs, :, HW:CW], lsem.at[2 * d + 1]),
+            ]
+            for load in more:
+                load.start()
+            loads += more
+        for load in loads:
+            load.wait()
 
     def forward(n):
         for d in range(1, 4):
@@ -290,15 +353,17 @@
             for d in range(4):
                 ac(n, d).wait_recv()
             chunk = tok[n].reshape(8 * TOK, CW)
-            for xp in range(4):
-                rows = places[xp * 4 : xp * 4 + 4].reshape(4 * SLAB, 8 * TOK)
+            for d in (1, 2, 3, 0):
+                xp = plus(x, d)
+                rows = places[pl.ds(xp * 4, 4)].reshape(4 * SLAB, 8 * TOK)
                 packed = jnp.dot(rows, chunk, preferred_element_type=f32).astype(bf16)
                 packed = packed.reshape(4, SLAB, CW)
                 sa[n, xp] = packed[:, :, :HW]
                 sb[n, :, xp] = packed[:, :, HW:]
+                if d > 0:
+                    p1_x(n, d).start()
             for d in range(1, 4):
-                for copy in p1(n, d):
-                    copy.start()
+                p1_z(n, d).start()
             for copy in own(n):
                 copy.start()
 
@@ -318,8 +383,19 @@
                     copy.wait_recv()
             for copy in own(i):
                 copy.wait()
-            for d in range(1, 4):
-                for copy in p2(i, d):
+
+            @pl.when(i < NS - 1)
+            def _():
+                for d in range(1, 4):
+                    for copy in p2(i, d):
+                        copy.start()
+
+            @pl.when(i == NS - 1)
+            def _():
+                for d in range(1, 4):
+                    for copy in p2_last(d):
+                        copy.start()
+                for copy in own_last():
                     copy.start()
 
             @pl.when(i < NF)
@@ -339,54 +415,34 @@
         @pl.when(n >= OUT_AHEAD + 2)
         def _():
             m = n - OUT_AHEAD - 2
-            swapped = (m == NS - 1) | (m == NS + 1)
-            first = pltpu.make_async_copy
+            swapped = (m == 3) | (m == 5)
+            own_step = jnp.where(m < 3, m, m // 2 + 1)
+            swap_step = (m - 3) // 2
 
             @pl.when(jnp.logical_not(swapped))
             def _():
-                i = jnp.minimum(m, NS - 1)
-                loads = [
-                    first(ma.at[i, z], xv.at[z, :, :, 0:HW], lsem.at[0]),
-                    first(mb.at[i, x], xv.at[:, x, :, HW:CW], lsem.at[1]),
-                ]
-                for load in loads:
-                    load.start()
-                for d in range(1, 4):
-                    @pl.when(i >= NF)
-                    def _():
-                        for copy in p2(i, d):
-                            copy.wait_recv()
-
-                    zs, xs = plus(z, 4 - d), plus(x, 4 - d)
-                    more = [
-                        first(xa.at[i, zs], xv.at[zs, :, :, 0:HW], lsem.at[2 * d]),
-                        first(xb.at[i, xs], xv.at[:, xs, :, HW:CW], lsem.at[2 * d + 1]),
-                    ]
-                    for load in more:
-                        load.start()
-                    loads += more
-                for load in loads:
-                    load.wait()
+                fetch(own_step, own_step >= NF)
 
             @pl.when(swapped)
             def _():
-                i = (m - NS + 1) // 2
+                i = swap_step
                 for d in range(4):
                     for copy in swap(i, d):
                         copy.wait_recv()
                 loads = []
                 for d in range(4):
                     loads += [
-                        first(pa.at[i, d], xv.at[d, :, :, 0:HW], lsem.at[2 * d]),
-                        first(pb.at[i, d], xv.at[:, d, :, HW:CW], lsem.at[2 * d + 1]),
+                        local(pa.at[i, d], xv.at[d, :, :, 0:HW], lsem.at[2 * d]),
+                        local(pb.at[i, d], xv.at[:, d, :, HW:CW], lsem.at[2 * d + 1]),
                     ]
                 for load in loads:
                     load.start()
                 for load in loads:
                     load.wait()
 
-            i = jnp.where(swapped, (m - NS + 1) // 2, jnp.minimum(m, NS - 1))
-            chunk = fetched(i, jnp.where(swapped, 1 - parity, parity))
+            chunk = fetched(
+                jnp.where(swapped, swap_step, own_step), jnp.where(swapped, 1 - parity, parity)
+            )
             for i in range(4):
                 rows = xv[i].reshape(4 * SLAB, CW)
                 gate[i] += jnp.dot(rows, wg[chunk], preferred_element_type=f32)
@@ -394,10 +450,20 @@
 
         return carry
 
-    lax.fori_loop(0, NQ + OUT_AHEAD + 2, step, 0)
+    lax.fori_loop(0, NQ + OUT_AHEAD + 1, step, 0)
+    for copy in own_last():
+        copy.wait()
+    for d in range(1, 4):
+        for copy in p2_last(d):
+            copy.wait_recv()
+    results = []
     for i in range(4):
-        value = gate[i]
-        inner_out[i] = (value / (1.0 + jnp.exp(-value)) * up[i]).astype(bf16)
+        rows = xlast[i].reshape(4 * SLAB, CW)
+        value = gate[i] + jnp.dot(rows, wg[NQ - 1], preferred_element_type=f32)
+        other = up[i] + jnp.dot(rows, wu[NQ - 1], preferred_element_type=f32)
+        inner[i] = (value / (1.0 + jnp.exp(-value)) * other).astype(bf16)
+        results.append(pltpu.make_async_copy(inner.at[i], inner_out.at[i], isem.at[i]))
+        results[-1].start()
 
     def finish(n, carry):
         for d in range(1, 4):
@@ -414,12 +480,15 @@
             for copy in swap(n, d):
                 copy.wait_send()
     finish_attend()
+    save.wait()
+    for copy in results:
+        copy.wait()
 
 
 def return_kernel(
-    inner, meta, resid, wd_hbm,
+    inner_hbm, meta, resid_hbm, wd_hbm,
     out, ra, rb, ya, yb,
-    places, slots, weights, sr, sw_out, sw_in, wd, rv, total, half, core_in, mix, y_in,
+    inner, resid, isem, turned, places, slots, weights, sr, sw_out, sw_in, wd, rv, rlast, osem, total, half, core_in, mix, y_in,
     p1_ss, p1_rs, p2_ss, p2_rs, rc_ss, rc_rs, ry_ss, ry_rs, sw_ss, sw_rs, loc, wsem, lsem,
 ):
     x, c, z, y = coords()
@@ -429,7 +498,13 @@
     zpeer = [place(x, c, plus(z, d), y) for d in range(1, 4)]
     load_wd = pltpu.make_async_copy(wd_hbm, wd, wsem)
     load_wd.start()
-    greet([core] + ypeer + xpeer + zpeer)
+    load_inner = [
+        pltpu.make_async_copy(inner_hbm.at[i], inner.at[i], isem.at[i]) for i in range(4)
+    ]
+    for load in load_inner:
+        load.start()
+    load_resid = pltpu.make_async_copy(resid_hbm, resid, isem.at[4])
+    load_resid.start()
 
     def p1_z(n, d):
         zp = plus(z, d)
@@ -437,12 +512,14 @@
             sr.at[n, zp, :, :, 0:HW], ra.at[n, :, z], p1_ss.at[n, 0, d - 1], p1_rs.at[n, 0, d - 1], zpeer[d - 1]
         )
 
+    def p1_x(n, d):
+        xp = plus(x, d)
+        return remote(
+            sr.at[n, :, xp, :, HW:CW], rb.at[n, :, x], p1_ss.at[n, 1, d - 1], p1_rs.at[n, 1, d - 1], xpeer[d - 1]
+        )
+
     def p1(n, d):
-        xp = plus(x, d)
-        return (
-            p1_z(n, d),
-            remote(sr.at[n, :, xp, :, HW:CW], rb.at[n, :, x], p1_ss.at[n, 1, d - 1], p1_rs.at[n, 1, d - 1], xpeer[d - 1]),
-        )
+        return p1_z(n, d), p1_x(n, d)
 
     def p1_part(n, i, d):
         xp = plus(x, d)
@@ -463,6 +540,20 @@
             remote(rb.at[n, zp], yb.at[n, z], p2_ss.at[n, 1, d - 1], p2_rs.at[n, 1, d - 1], zpeer[d - 1]),
         )
 
+    def p2_last(d):
+        n, xp, zp = NS - 1, plus(x, d), plus(z, d)
+        return (
+            remote(ra.at[n, xp], rlast.at[x, :, :, 0:HW], p2_ss.at[n, 0, d - 1], p2_rs.at[n, 0, d - 1], xpeer[d - 1]),
+            remote(rb.at[n, zp], rlast.at[:, z, :, HW:CW], p2_ss.at[n, 1, d - 1], p2_rs.at[n, 1, d - 1], zpeer[d - 1]),
+        )
+
+    def own_last():
+        n = NS - 1
+        return (
+            pltpu.make_async_copy(ra.at[n, x], rlast.at[x, :, :, 0:HW], osem.at[0]),
+            pltpu.make_async_copy(rb.at[n, z], rlast.at[:, z, :, HW:CW], osem.at[1]),
+        )
+
     def rc(n):
         return remote(
             half.at[lax.rem(n, 2), 1 - c], core_in.at[n], rc_ss.at[n], rc_rs.at[n], core
@@ -499,22 +590,34 @@
 
     order = (1, 2, 3, 0)
 
-    def start_swap(f):
+    def fill_swap(f, d):
+        i = plus(z, d)
+        part = down(i, 2 * f + 1 - parity).astype(bf16)
+        sw_out[f, i] = part.reshape(4, SLAB, CW)
+
+    load_wd.wait()
+    for load in load_inner:
+        load.wait()
+    def fill_step(n):
         for d in order:
             i = plus(z, d)
-            part = down(i, 2 * f + 1 - parity).astype(bf16)
-            sw_out[f, i] = part.reshape(4, SLAB, CW)
-            swap(f, d).start()
-
-    load_wd.wait()
-    start_swap(0)
+            part = down(i, 2 * NF + n)
+            sr[n, i] = part.astype(bf16).reshape(4, SLAB, CW)
+
+    for d in order:
+        fill_swap(0, d)
+    fill_step(0)
+    greet([core] + ypeer + xpeer + zpeer)
+    for d in order:
+        swap(0, d).start()
 
     def step(n, carry):
         @pl.when(n < NS - NF)
         def _():
-            for i in range(4):
-                part = down(i, 2 * NF + n)
-                sr[n, i] = part.astype(bf16).reshape(4, SLAB, CW)
+            @pl.when(n > 0)
+            def _():
+                fill_step(n)
+
             for d in range(1, 4):
                 for copy in p1(n, d):
                     copy.start()
@@ -524,9 +627,14 @@
         @pl.when(n == 0)
         def _():
             for f in range(1, NF):
-                start_swap(f)
+                for d in order:
+                    fill_swap(f, d)
+                    swap(f, d).start()
             find_slots(meta, slots, weights, c, y)
             fill_places(slots, weights, places)
+            for i in range(2):
+                group = places[8 * i : 8 * i + 8].reshape(8 * SLAB, 8 * TOK)
+                turned[:, 8 * SLAB * i : 8 * SLAB * (i + 1)] = group.T
 
         @pl.when((n >= BACK_AHEAD) & (n < NS + BACK_AHEAD))
         def _():
@@ -536,8 +644,19 @@
                     copy.wait_recv()
             for copy in own(i):
                 copy.wait()
-            for d in range(1, 4):
-                for copy in p2(i, d):
+
+            @pl.when(i < NS - 1)
+            def _():
+                for d in range(1, 4):
+                    for copy in p2(i, d):
+                        copy.start()
+
+            @pl.when(i == NS - 1)
+            def _():
+                for d in range(1, 4):
+                    for copy in p2_last(d):
+                        copy.start()
+                for copy in own_last():
                     copy.start()
 
         @pl.when((n >= 4) & (n < NS + 4))
@@ -564,32 +683,44 @@
         @pl.when((n >= 3) & (n < NS + 3))
         def _():
             m = n - 3
-            loads = [
-                pltpu.make_async_copy(ra.at[m, x], rv.at[x, :, :, 0:HW], lsem.at[0]),
-                pltpu.make_async_copy(rb.at[m, z], rv.at[:, z, :, HW:CW], lsem.at[1]),
-            ]
-            for load in loads:
-                load.start()
-            for d in range(1, 4):
-                for copy in p2(m, d):
-                    copy.wait_recv()
-                zs, xs = plus(z, 4 - d), plus(x, 4 - d)
-                more = [
-                    pltpu.make_async_copy(ya.at[m, xs], rv.at[xs, :, :, 0:HW], lsem.at[2 * d]),
-                    pltpu.make_async_copy(yb.at[m, zs], rv.at[:, zs, :, HW:CW], lsem.at[2 * d + 1]),
+
+            def combine(rows):
+                moe = jnp.dot(
+                    turned[...], rows[...].reshape(16 * SLAB, CW), preferred_element_type=f32
+                )
+                total[lax.rem(m, 2)] = moe.reshape(2, 4, TOK, CW)
+
+            @pl.when(m < NS - 1)
+            def _():
+                loads = [
+                    pltpu.make_async_copy(ra.at[m, x], rv.at[x, :, :, 0:HW], lsem.at[0]),
+                    pltpu.make_async_copy(rb.at[m, z], rv.at[:, z, :, HW:CW], lsem.at[1]),
                 ]
-                for load in more:
+                for load in loads:
                     load.start()
-                loads += more
-            for load in loads:
-                load.wait()
-            moe = lax.dot_general(
-                places[...].reshape(16 * SLAB, 8 * TOK),
-                rv[...].reshape(16 * SLAB, CW),
-                (((0,), (0,)), ((), ())),
-                preferred_element_type=f32,
-            )
-            total[lax.rem(m, 2)] = moe.reshape(2, 4, TOK, CW)
+                for d in range(1, 4):
+                    for copy in p2(m, d):
+                        copy.wait_recv()
+                    zs, xs = plus(z, 4 - d), plus(x, 4 - d)
+                    more = [
+                        pltpu.make_async_copy(ya.at[m, xs], rv.at[xs, :, :, 0:HW], lsem.at[2 * d]),
+                        pltpu.make_async_copy(yb.at[m, zs], rv.at[:, zs, :, HW:CW], lsem.at[2 * d + 1]),
+                    ]
+                    for load in more:
+                        load.start()
+                    loads += more
+                for load in loads:
+                    load.wait()
+                combine(rv)
+
+            @pl.when(m == NS - 1)
+            def _():
+                for copy in own_last():
+                    copy.wait()
+                for d in range(1, 4):
+                    for copy in p2_last(d):
+                        copy.wait_recv()
+                combine(rlast)
 
             @pl.when(m >= 2)
             def _():
@@ -617,6 +748,7 @@
         return carry
 
     lax.fori_loop(0, NS + 4, step, 0)
+    load_resid.wait()
 
     def result(m, carry):
         for d in range(1, 4):
@@ -683,14 +815,19 @@
             jax.ShapeDtypeStruct((8, 2 * TOPK, TOK), f32),
             jax.ShapeDtypeStruct((4, 4 * SLAB, FF_HALF), bf16),
         ) + (landing,) * 4 + (swapped,) * 2,
-        in_specs=[VM] * 8 + [ANY] * 2,
-        out_specs=(VM,) * 3 + (ANY,) * 6,
+        in_specs=[ANY] * 2 + [VM] * 6 + [ANY] * 2,
+        out_specs=(ANY, VM, ANY) + (ANY,) * 6,
         scratch_shapes=[
             pltpu.VMEM((KV_HEADS, WINDOW, TOK, HEAD_DIM), bf16),
             pltpu.VMEM((KV_HEADS, WINDOW, TOK, HEAD_DIM), bf16),
             pltpu.VMEM((WINDOW, 8, TOK), f32),
             pltpu.VMEM((2 * TOPK, TOK), f32),
             dma(KV_HEADS, 3, 2), dma(KV_HEADS, 3, 2), dma(3), dma(3), dma(7), dma(7),
+            pltpu.VMEM((TOK, D), bf16),
+            pltpu.VMEM((TOK, D), bf16),
+            pltpu.VMEM((TOK, D), bf16),
+            pltpu.VMEM((4, 4 * SLAB, FF_HALF), bf16),
+            dma(4), dma(3), dma(2),
             pltpu.VMEM((NQ, TOK, CW), bf16),
             pltpu.VMEM((NS, 8, TOK, CW), bf16),
             pltpu.VMEM((16, SLAB, 8 * TOK), bf16),
@@ -702,6 +839,7 @@
             pltpu.VMEM((NQ, CW, FF_HALF), bf16),
             pltpu.VMEM((NQ, CW, FF_HALF), bf16),
             pltpu.VMEM((4, 4, SLAB, CW), bf16),
+            pltpu.VMEM((4, 4, SLAB, CW), bf16),
             dma(NS, 3), dma(NS, 3), dma(NS, 4), dma(NS, 4),
             dma(NS, 2, 3), dma(NS, 2, 3), dma(NS, 2, 3), dma(NS, 2, 3),
             dma(NF, 2, 4), dma(NF, 2, 4), dma(NS, 2), dma(2), dma(8),
@@ -709,16 +847,20 @@
         compiler_params=params(0),
     )(
         hidden_in, queries, key_rows, value_rows, document_ids.reshape(1, TOK), expert_ids.T,
-        route_weights.T, norm_gain.reshape(1, D),
+        route_weights.T, norm_gain.reshape(D // HEAD_DIM, HEAD_DIM),
         w_gate.reshape(NQ, CW, FF_HALF), w_up.reshape(NQ, CW, FF_HALF),
     )
 
     out, *_ = pl.pallas_call(
         return_kernel,
         out_shape=(jax.ShapeDtypeStruct((TOK, D), bf16),) + (landing,) * 4,
-        in_specs=[VM, VM, VM, ANY],
+        in_specs=[ANY, VM, ANY, ANY],
         out_specs=(VM,) + (ANY,) * 4,
         scratch_shapes=[
+            pltpu.VMEM((4, 4 * SLAB, FF_HALF), bf16),
+            pltpu.VMEM((TOK, D), bf16),
+            dma(5),
+            pltpu.VMEM((8 * TOK, 16 * SLAB), bf16),
             pltpu.VMEM((16, SLAB, 8 * TOK), bf16),
             pltpu.VMEM((16, 8, TOK), f32),
             pltpu.VMEM((16, 8, TOK), f32),
@@ -727,6 +869,8 @@
             pltpu.VMEM((NF, 4, 4, SLAB, CW), bf16),
             pltpu.VMEM((FF_HALF, D), bf16),
             pltpu.VMEM((4, 4, SLAB, CW), bf16),
+            pltpu.VMEM((4, 4, SLAB, CW), bf16),
+            dma(2),
             pltpu.VMEM((2, 2, 4, TOK, CW), f32),
             pltpu.VMEM((2, 2, 4, TOK, CW), bf16),
             pltpu.VMEM((NS, 4, TOK, CW), bf16),

time: 356 us -> 346 us (0.972)
  Pallas kernels: 352 us -> 343 us
    pallas_call x1, Pallas kernels: 188 us -> 183 us  [on_device(): pl.pallas_call(expert_kernel, out_shape=(jax.ShapeDtypeStruct((TOK, D), b...]
where the time goes in v4:
time: 346 us
  Pallas kernels  343 us (99%)
    pallas_call x1, Pallas kernels, on_device(): pl.pallas_call(expert_kernel, out_shape=(jax.ShapeDtypeStruct((TOK, D), b...  183 us
    pallas_call x1, Pallas kernels, on_device(): pl.pallas_call(return_kernel, out_shape=(jax.ShapeDtypeStruct((TOK, D), b...  160 us

profile of v4, /device:TPU:0, one launch (start us, length us, event | category | flops | bytes accessed | tf_op | source)
XLA Modules:
  0.0 345.6 jit_solution(5752519122316431691)
XLA Ops:
  0.0 182.9 %shard_map.109 = (bf16[128,3584]{1,0:T(8,128)(2,1)}, f32[8,16,128]{2,1,0:T(8,128)}, bf16[4,576,640]{2,1,0:T(8,128)(2,1)}, bf16[5,4,4,144,256]{4,3,2,1,0:T(8,128)...) custom-call(bf16[128,3584]{1,0:T(8,128)(2,1)} %hid_hbm.1, ...), custom_call_target="tpu_custom_call" | custom-call | tf_op jit(solution)/shard_map/pallas_call | solution.py:811
  183.0 160.5 %shard_map.110 = (bf16[128,3584]{1,0:T(8,128)(2,1)}, bf16[5,4,4,144,256]{4,3,2,1,0:T(8,128)(2,1)}, bf16[5,4,4,144,256]{4,3,2,1,0:T(8,128)(2,1)}, bf16[5,4,4,144,...) custom-call(bf16[4,576,640]{2,1,0:T(8,128)(2,1)} %get-tuple-element.9.inner_hbm, f32[8,16,128]{2,1,0:T(8,128)} %get-tuple-element.10.meta, ...), custom_call_target="tpu_custom_call" | custom-call | tf_op jit(solution)/shard_map/pallas_call | solution.py:854
  343.4 2.2 copy.13

commit v5 on v4

--- a/solution.py
+++ b/solution.py
@@ -66,7 +66,7 @@
 
 def attend(
     x, c, z, y, rank, hid, q, k, v, doc, ids, route, gain, resid_out, nrm, meta_all,
-    kw, vw, docw, meta, halo_ss, halo_rs, doc_ss, doc_rs, meta_ss, meta_rs, by_rank, peers, fills,
+    kw, vw, docw, meta, halo_ss, halo_rs, doc_ss, doc_rs, meta_ss, meta_rs, by_rank, peers, fills, when_first,
 ):
     mine = c * 4 + y
     row = jnp.broadcast_to(doc[...].astype(f32), (TOK, TOK))
@@ -149,6 +149,8 @@
             value = resid_out[:, at : at + HEAD_DIM].astype(f32) * inverse
             tile = n * (CW // HEAD_DIM) + j
             nrm[n, :, j * HEAD_DIM : (j + 1) * HEAD_DIM] = (value * gain[tile : tile + 1, :]).astype(bf16)
+        if n == 1:
+            when_first()
     for i in range(7):
         send_meta(i).wait_recv()
 
@@ -228,12 +230,6 @@
         copy.start()
 
     greet([by_rank(d) for d in (1, 2, 3, -1, -2, -3)] + peers + xpeer + zpeer)
-    finish_attend = attend(
-        x, c, z, y, rank, hid, q, k, v, doc, ids, route, gain, resid, nrm, meta_all,
-        kw, vw, docw, meta, halo_ss, halo_rs, doc_ss, doc_rs, meta_ss, meta_rs, by_rank, peers, fills,
-    )
-    save = pltpu.make_async_copy(resid, resid_out, rsem.at[2])
-    save.start()
     mine = c * 4 + y
     parity = lax.rem(y, 2)
     pair = place(x, c, z, y + 1 - 2 * parity)
@@ -300,12 +296,17 @@
         )
 
     def start_gather(n):
-        for d in range(1, 4):
+        for d in (2, 1, 3):
             ay(n, d).start()
         ac(n, 0).start()
         tok[n, mine] = nrm[fetched(n, parity)]
 
-    start_gather(0)
+    finish_attend = attend(
+        x, c, z, y, rank, hid, q, k, v, doc, ids, route, gain, resid, nrm, meta_all,
+        kw, vw, docw, meta, halo_ss, halo_rs, doc_ss, doc_rs, meta_ss, meta_rs, by_rank, peers, fills, lambda: start_gather(0),
+    )
+    save = pltpu.make_async_copy(resid, resid_out, rsem.at[2])
+    save.start()
 
     local = pltpu.make_async_copy
 
@@ -320,7 +321,7 @@
         ]
         for load in loads:
             load.start()
-        for d in range(1, 4):
+        for d in (2, 1, 3):
             pl.when(arriving)(lambda: arrive(d))
             zs, xs = plus(z, 4 - d), plus(x, 4 - d)
             more = [
@@ -334,7 +335,7 @@
             load.wait()
 
     def forward(n):
-        for d in range(1, 4):
+        for d in (2, 1, 3):
             ay(n, d).wait_recv()
             ac(n, d).start()
 
@@ -353,7 +354,7 @@
             for d in range(4):
                 ac(n, d).wait_recv()
             chunk = tok[n].reshape(8 * TOK, CW)
-            for d in (1, 2, 3, 0):
+            for d in (2, 1, 3, 0):
                 xp = plus(x, d)
                 rows = places[pl.ds(xp * 4, 4)].reshape(4 * SLAB, 8 * TOK)
                 packed = jnp.dot(rows, chunk, preferred_element_type=f32).astype(bf16)
@@ -362,7 +363,7 @@
                 sb[n, :, xp] = packed[:, :, HW:]
                 if d > 0:
                     p1_x(n, d).start()
-            for d in range(1, 4):
+            for d in (2, 1, 3):
                 p1_z(n, d).start()
             for copy in own(n):
                 copy.start()
@@ -378,7 +379,7 @@
         @pl.when((n >= OUT_AHEAD) & (n < NS + OUT_AHEAD))
         def _():
             i = n - OUT_AHEAD
-            for d in range(1, 4):
+            for d in (2, 1, 3):
                 for copy in p1(i, d):
                     copy.wait_recv()
             for copy in own(i):
@@ -386,13 +387,13 @@
 
             @pl.when(i < NS - 1)
             def _():
-                for d in range(1, 4):
+                for d in (2, 1, 3):
                     for copy in p2(i, d):
                         copy.start()
 
             @pl.when(i == NS - 1)
             def _():
-                for d in range(1, 4):
+                for d in (2, 1, 3):
                     for copy in p2_last(d):
                         copy.start()
                 for copy in own_last():
@@ -406,7 +407,7 @@
         @pl.when((n > OUT_AHEAD) & (n <= OUT_AHEAD + NF))
         def _():
             i = n - OUT_AHEAD - 1
-            for d in range(1, 4):
+            for d in (2, 1, 3):
                 for copy in p2(i, d):
                     copy.wait_recv()
                 for copy in swap(i, d):
@@ -453,7 +454,7 @@
     lax.fori_loop(0, NQ + OUT_AHEAD + 1, step, 0)
     for copy in own_last():
         copy.wait()
-    for d in range(1, 4):
+    for d in (2, 1, 3):
         for copy in p2_last(d):
             copy.wait_recv()
     results = []
@@ -466,7 +467,7 @@
         results[-1].start()
 
     def finish(n, carry):
-        for d in range(1, 4):
+        for d in (2, 1, 3):
             ay(n, d).wait_send()
             for copy in p1(n, d) + p2(n, d):
                 copy.wait_send()
@@ -488,7 +489,7 @@
 def return_kernel(
     inner_hbm, meta, resid_hbm, wd_hbm,
     out, ra, rb, ya, yb,
-    inner, resid, isem, turned, places, slots, weights, sr, sw_out, sw_in, wd, rv, rlast, osem, total, half, core_in, mix, y_in,
+    inner, resid, isem, turned, places, slots, weights, sa, sb, sw_out, sw_in, wd, rv, rlast, osem, total, half, core_in, mix, y_in,
     p1_ss, p1_rs, p2_ss, p2_rs, rc_ss, rc_rs, ry_ss, ry_rs, sw_ss, sw_rs, loc, wsem, lsem,
 ):
     x, c, z, y = coords()
@@ -509,13 +510,13 @@
     def p1_z(n, d):
         zp = plus(z, d)
         return remote(
-            sr.at[n, zp, :, :, 0:HW], ra.at[n, :, z], p1_ss.at[n, 0, d - 1], p1_rs.at[n, 0, d - 1], zpeer[d - 1]
+            sa.at[n, zp], ra.at[n, :, z], p1_ss.at[n, 0, d - 1], p1_rs.at[n, 0, d - 1], zpeer[d - 1]
         )
 
     def p1_x(n, d):
         xp = plus(x, d)
         return remote(
-            sr.at[n, :, xp, :, HW:CW], rb.at[n, :, x], p1_ss.at[n, 1, d - 1], p1_rs.at[n, 1, d - 1], xpeer[d - 1]
+            sb.at[n, xp], rb.at[n, :, x], p1_ss.at[n, 1, d - 1], p1_rs.at[n, 1, d - 1], xpeer[d - 1]
         )
 
     def p1(n, d):
@@ -524,13 +525,13 @@
     def p1_part(n, i, d):
         xp = plus(x, d)
         return remote(
-            sr.at[n, i, xp, :, HW:CW], rb.at[n, i, x], p1_ss.at[n, 1, d - 1], p1_rs.at[n, 1, d - 1], xpeer[d - 1]
+            sb.at[n, xp, i], rb.at[n, i, x], p1_ss.at[n, 1, d - 1], p1_rs.at[n, 1, d - 1], xpeer[d - 1]
         )
 
     def own(n):
         return (
-            pltpu.make_async_copy(sr.at[n, z, :, :, 0:HW], ra.at[n, :, z], loc.at[n, 0]),
-            pltpu.make_async_copy(sr.at[n, :, x, :, HW:CW], rb.at[n, :, x], loc.at[n, 1]),
+            pltpu.make_async_copy(sa.at[n, z], ra.at[n, :, z], loc.at[n, 0]),
+            pltpu.make_async_copy(sb.at[n, x], rb.at[n, :, x], loc.at[n, 1]),
         )
 
     def p2(n, d):
@@ -588,7 +589,7 @@
         cols = pl.ds(pl.multiple_of(chunk * CW, CW), CW)
         return jnp.dot(inner[i], wd[:, cols], preferred_element_type=f32)
 
-    order = (1, 2, 3, 0)
+    order = (2, 1, 3, 0)
 
     def fill_swap(f, d):
         i = plus(z, d)
@@ -601,8 +602,9 @@
     def fill_step(n):
         for d in order:
             i = plus(z, d)
-            part = down(i, 2 * NF + n)
-            sr[n, i] = part.astype(bf16).reshape(4, SLAB, CW)
+            part = down(i, 2 * NF + n).astype(bf16).reshape(4, SLAB, CW)
+            sa[n, i] = part[:, :, :HW]
+            sb[n, :, i] = part[:, :, HW:]
 
     for d in order:
         fill_swap(0, d)
@@ -618,7 +620,7 @@
             def _():
                 fill_step(n)
 
-            for d in range(1, 4):
+            for d in (2, 1, 3):
                 for copy in p1(n, d):
                     copy.start()
             for copy in own(n):
@@ -639,7 +641,7 @@
         @pl.when((n >= BACK_AHEAD) & (n < NS + BACK_AHEAD))
         def _():
             i = n - BACK_AHEAD
-            for d in range(1, 4):
+            for d in (2, 1, 3):
                 for copy in p1(i, d):
                     copy.wait_recv()
             for copy in own(i):
@@ -647,18 +649,36 @@
 
             @pl.when(i < NS - 1)
             def _():
-                for d in range(1, 4):
+                for d in (2, 1, 3):
                     for copy in p2(i, d):
                         copy.start()
 
             @pl.when(i == NS - 1)
             def _():
-                for d in range(1, 4):
+                for d in (2, 1, 3):
                     for copy in p2_last(d):
                         copy.start()
                 for copy in own_last():
                     copy.start()
 
+        @pl.when((n == NS - NF) | (n == NS))
+        def _():
+            f = (n - (NS - NF)) // 2
+            u = NS - NF + f
+            for d in order:
+                swap(f, d).wait_recv()
+                i = plus(z, d)
+                part = down(i, 2 * f + parity).reshape(4, SLAB, CW)
+                part = (part + sw_in[f, i].astype(f32)).astype(bf16)
+                sa[u, i] = part[:, :, :HW]
+                sb[u, :, i] = part[:, :, HW:]
+                if d > 0:
+                    p1_z(u, d).start()
+                for e in range(1, 4):
+                    p1_part(u, i, e).start()
+            for copy in own(u):
+                copy.start()
+
         @pl.when((n >= 4) & (n < NS + 4))
         def _():
             m = n - 4
@@ -677,7 +697,7 @@
 
             @pl.when(m >= 2)
             def _():
-                for d in range(1, 4):
+                for d in (2, 1, 3):
                     ry(m, d).start()
 
         @pl.when((n >= 3) & (n < NS + 3))
@@ -698,7 +718,7 @@
                 ]
                 for load in loads:
                     load.start()
-                for d in range(1, 4):
+                for d in (2, 1, 3):
                     for copy in p2(m, d):
                         copy.wait_recv()
                     zs, xs = plus(z, 4 - d), plus(x, 4 - d)
@@ -717,7 +737,7 @@
             def _():
                 for copy in own_last():
                     copy.wait()
-                for d in range(1, 4):
+                for d in (2, 1, 3):
                     for copy in p2_last(d):
                         copy.wait_recv()
                 combine(rlast)
@@ -729,29 +749,13 @@
             half[lax.rem(m, 2)] = total[lax.rem(m, 2)].astype(bf16)
             rc(m).start()
 
-        @pl.when((n == NS - NF) | (n == NS))
-        def _():
-            f = (n - (NS - NF)) // 2
-            u = NS - NF + f
-            for d in order:
-                swap(f, d).wait_recv()
-                i = plus(z, d)
-                part = down(i, 2 * f + parity).reshape(4, SLAB, CW)
-                sr[u, i] = (part + sw_in[f, i].astype(f32)).astype(bf16)
-                if d > 0:
-                    p1_z(u, d).start()
-                for e in range(1, 4):
-                    p1_part(u, i, e).start()
-            for copy in own(u):
-                copy.start()
-
         return carry
 
     lax.fori_loop(0, NS + 4, step, 0)
     load_resid.wait()
 
     def result(m, carry):
-        for d in range(1, 4):
+        for d in (2, 1, 3):
             ry(m, d).wait_recv()
         own_part = mix[m, y].astype(f32)
         one, two, three = [y_in[m, i].astype(f32) for i in range(3)]
@@ -774,7 +778,7 @@
     lax.fori_loop(0, NS, result, 0)
 
     def finish(n, carry):
-        for d in range(1, 4):
+        for d in (2, 1, 3):
             for copy in p1(n, d) + p2(n, d):
                 copy.wait_send()
             ry(n, d).wait_send()
@@ -864,7 +868,8 @@
             pltpu.VMEM((16, SLAB, 8 * TOK), bf16),
             pltpu.VMEM((16, 8, TOK), f32),
             pltpu.VMEM((16, 8, TOK), f32),
-            pltpu.VMEM((NS, 4, 4, SLAB, CW), bf16),
+            pltpu.VMEM((NS, 4, 4, SLAB, HW), bf16),
+            pltpu.VMEM((NS, 4, 4, SLAB, HW), bf16),
             pltpu.VMEM((NF, 4, 4, SLAB, CW), bf16),
             pltpu.VMEM((NF, 4, 4, SLAB, CW), bf16),
             pltpu.VMEM((FF_HALF, D), bf16),

time: 346 us -> 345 us (level)
  no operation moved by 1% of the time
where the time goes in v5:
time: 345 us; the launch traced here: 344 us
  Pallas kernels  342 us (99%)
    pallas_call x1, Pallas kernels, on_device(): pl.pallas_call(expert_kernel, out_shape=(jax.ShapeDtypeStruct((TOK, D), b...  183 us
    pallas_call x1, Pallas kernels, on_device(): pl.pallas_call(return_kernel, out_shape=(jax.ShapeDtypeStruct((TOK, D), b...  159 us

profile of v5, /device:TPU:0, one launch (start us, length us, event | category | flops | bytes accessed | tf_op | source)
XLA Modules:
  0.0 344.0 jit_solution(9396122400652762933)
XLA Ops:
  0.0 183.1 %shard_map.109 = (bf16[128,3584]{1,0:T(8,128)(2,1)}, f32[8,16,128]{2,1,0:T(8,128)}, bf16[4,576,640]{2,1,0:T(8,128)(2,1)}, bf16[5,4,4,144,256]{4,3,2,1,0:T(8,128)...) custom-call(bf16[128,3584]{1,0:T(8,128)(2,1)} %hid_hbm.1, ...), custom_call_target="tpu_custom_call" | custom-call | tf_op jit(solution)/shard_map/pallas_call | solution.py:815
  183.1 158.7 %shard_map.110 = (bf16[128,3584]{1,0:T(8,128)(2,1)}, bf16[5,4,4,144,256]{4,3,2,1,0:T(8,128)(2,1)}, bf16[5,4,4,144,256]{4,3,2,1,0:T(8,128)(2,1)}, bf16[5,4,4,144,...) custom-call(bf16[4,576,640]{2,1,0:T(8,128)(2,1)} %get-tuple-element.9.inner_hbm, f32[8,16,128]{2,1,0:T(8,128)} %get-tuple-element.10.meta, ...), custom_call_target="tpu_custom_call" | custom-call | tf_op jit(solution)/shard_map/pallas_call | solution.py:858
  341.8 2.2 copy.13
